TPU v7x, 32 devices: a whole 2x2x4 slice. The times are simulated.
32 devices in a mesh: groups: 2 (over y), tensor: 4 (over z), dp: 4 (over x, core).
Axes of the slice: x: 2, y: 2, z: 4, core: 2. Of those that a mesh axis runs over, the one named last changes fastest.
Arguments:
- tokens_in: bfloat16 [1024, 4096], P(('groups', 'dp'), 'tensor'), parts along dimension 0, may hold values from -6 to 6
- hidden_grad: bfloat16 [1024, 112, 128], P(('groups', 'dp'), 'tensor'), parts along dimension 0, may hold values from -6 to 6
- gate_blocks: bfloat16 [112, 16, 128, 128], P('tensor'), may hold values from -0.125 to 0.125
- up_blocks: bfloat16 [112, 16, 128, 128], P('tensor'), may hold values from -0.125 to 0.125
- gate_rows: int32 [112, 16], replicated, may hold values from 0 to 31, as said below
- up_rows: int32 [112, 16], replicated, may hold values from 0 to 31, as said below
- column_of_slot: int32 [112], P('tensor'), may hold values from 0 to 111, as said below
Outputs:
- tokens_grad: bfloat16 [1024, 4096], P(('groups', 'dp'), 'tensor'), parts along dimension 0
- gate_grad: bfloat16 [112, 32, 128, 128], P('tensor', ('groups', 'dp')), parts along dimension 1
- up_grad: bfloat16 [112, 32, 128, 128], P('tensor', ('groups', 'dp')), parts along dimension 1
There are 2 independent parts, one for each index of `groups`. A program takes and returns all parts, laid end to end along the dimension named above; an argument that names none is the same for every part. Nothing has to cross between parts.
Inputs may be any that keep to these rules, and one draw needn't show every extreme that they name: `gate_rows`: each row holds 16 distinct row blocks in rising order. `up_rows`: each row holds 16 distinct row blocks in rising order. `column_of_slot`: every column block 0 to 111 stands in exactly one slot; the other slots hold 112; slot s lies on tensor index s // 28.
All inputs are finite; a program needn't handle non-finite values.
Results may differ from a plain program's by a relative error of at most 0.009.
Values may be sent and summed in bfloat16 or wider, within the bound.
A program may use at most 384 MiB of HBM per device.

v0:
```python
import jax
import jax.numpy as jnp
from jax import lax
from jax.sharding import PartitionSpec as P


def body(tokens_in, hidden_grad, gate_blocks, up_blocks, gate_rows, up_rows, column_of_slot):
    token_count = tokens_in.shape[0]
    local_width = tokens_in.shape[1]
    slot_count = gate_blocks.shape[0]
    nonzero = gate_blocks.shape[1]
    block_side = gate_blocks.shape[2]
    column_count = gate_rows.shape[0]
    full_width = local_width * lax.axis_size("tensor")
    row_blocks = full_width // block_side
    column_hot = (
        column_of_slot[:, None] == jnp.arange(column_count, dtype=jnp.int32)[None, :]
    ).astype(jnp.int32)
    rows_gate = jnp.sum(column_hot[:, :, None] * gate_rows[None, :, :], axis=1)
    rows_up = jnp.sum(column_hot[:, :, None] * up_rows[None, :, :], axis=1)
    in_use = (column_of_slot < column_count).astype(jnp.float32)
    gathered = lax.all_gather(tokens_in, "tensor", axis=1, tiled=True)
    token_blocks = gathered.reshape(token_count, row_blocks, block_side)
    picked_gate = jnp.take(token_blocks, rows_gate.reshape(-1), axis=1).reshape(
        token_count, slot_count, nonzero, block_side
    )
    picked_up = jnp.take(token_blocks, rows_up.reshape(-1), axis=1).reshape(
        token_count, slot_count, nonzero, block_side
    )
    gate_value = jnp.einsum(
        "tsnb,snbc->tsc", picked_gate, gate_blocks, preferred_element_type=jnp.float32
    )
    up_value = jnp.einsum(
        "tsnb,snbc->tsc", picked_up, up_blocks, preferred_element_type=jnp.float32
    )
    masked = hidden_grad.astype(jnp.float32) * in_use[None, :, None]
    sigmoid_gate = jax.nn.sigmoid(gate_value)
    gate_cot = (
        masked * up_value * sigmoid_gate * (1.0 + gate_value * (1.0 - sigmoid_gate))
    ).astype(jnp.bfloat16)
    up_cot = (masked * gate_value * sigmoid_gate).astype(jnp.bfloat16)
    back_gate = jnp.einsum(
        "tsc,snbc->tsnb", gate_cot, gate_blocks, preferred_element_type=jnp.float32
    )
    back_up = jnp.einsum("tsc,snbc->tsnb", up_cot, up_blocks, preferred_element_type=jnp.float32)
    partial_value = jnp.zeros((token_count, row_blocks, block_side), jnp.float32)
    partial_value = partial_value.at[:, rows_gate.reshape(-1)].add(
        back_gate.reshape(token_count, slot_count * nonzero, block_side)
    )
    partial_value = partial_value.at[:, rows_up.reshape(-1)].add(
        back_up.reshape(token_count, slot_count * nonzero, block_side)
    )
    partial_value = partial_value.reshape(token_count, full_width)
    arrived = lax.all_to_all(
        partial_value.astype(jnp.bfloat16), "tensor", split_axis=1, concat_axis=0, tiled=True
    )
    tokens_grad = jnp.sum(
        arrived.reshape(-1, token_count, local_width).astype(jnp.float32), axis=0
    ).astype(jnp.bfloat16)
    part_gate = jnp.einsum(
        "tsnb,tsc->nsbc", picked_gate, gate_cot, preferred_element_type=jnp.float32
    )
    part_up = jnp.einsum("tsnb,tsc->nsbc", picked_up, up_cot, preferred_element_type=jnp.float32)
    summed = lax.psum_scatter(
        jnp.stack((part_gate, part_up), axis=1).astype(jnp.bfloat16),
        "dp",
        scatter_dimension=0,
        tiled=True,
    ).astype(jnp.float32)
    summed_gate = summed[:, 0].transpose(1, 0, 2, 3).astype(jnp.bfloat16)
    summed_up = summed[:, 1].transpose(1, 0, 2, 3).astype(jnp.bfloat16)
    return (tokens_grad, summed_gate, summed_up)


def solution(mesh):
    placed = (
        P(("groups", "dp"), "tensor"),
        P(("groups", "dp"), "tensor", None),
        P("tensor", None, None, None),
        P("tensor", None, None, None),
        P(),
        P(),
        P("tensor"),
    )
    return jax.shard_map(
        body,
        mesh=mesh,
        in_specs=placed,
        out_specs=(
            P(("groups", "dp"), "tensor"),
            P("tensor", ("groups", "dp"), None, None),
            P("tensor", ("groups", "dp"), None, None),
        ),
        check_vma=False,
    )
```

profile of v0, /device:TPU:0, one launch (start us, length us, event | category | flops | bytes accessed | tf_op | source)
XLA Modules:
  0.0 684.3 jit_solution(14692639016369690322)
XLA Ops:
  7.2 1.8 copy.46
  9.8 1.7 multiply_reduce_fusion
  12.4 28.4 %all-gather.2.cloned.1.call-done = bf16[128,4096]{0,1:T(8,128)(2,1)} async-done(((bf16[128,1024]{0,1:T(8,128)(2,1)}), bf16[128,4096]{0,1:T(8,128)(2,1)}) %all-gather.2.cloned.1.call-update) | async-done | bytes 1048592 | tf_op jit(solution)/shard_map/all_gather | solution.py:22
  40.8 1.6 copy.47
  42.4 13.1 %gather_fusion.1 = bf16[448,128,128]{2,1,0:T(8,128)(2,1)} fusion(bf16[128,32,128]{2,0,1:T(8,128)(2,1)S(1)} %copy.47, s32[1024]{0:T(1024)S(1)} %pad_clamp_fusion), kind=kCustom, calls=%fused_computation.1.clone | custom fusion | bytes 29361920 | tf_op jit(solution)/shard_map/jit(_take)/gather | solution.py:24
  55.6 13.3 %gather_fusion = bf16[448,128,128]{2,1,0:T(8,128)(2,1)} fusion(bf16[128,32,128]{2,0,1:T(8,128)(2,1)S(1)} %copy.47, s32[1024]{0:T(1024)S(1)} %pad_clamp_fusion.1), kind=kCustom, calls=%fused_computation.clone | custom fusion | bytes 29361920 | tf_op jit(solution)/shard_map/jit(_take)/gather | solution.py:27
  68.9 13.8 %broadcast_select_fusion = bf16[448,128,128]{2,1,0:T(8,128)(2,1)} fusion(bf16[448,128,128]{2,1,0:T(8,128)(2,1)} %gather_fusion.1, pred[448]{0:T(512)(128)(4,1)S(1)} %compare_and_fusion), kind=kLoop, calls=%fused_computation.7 | loop fusion | flops 7340032 | bytes 29360576 | tf_op jit(solution)/shard_map/jit(_take)/select_n | solution.py:24
  82.7 13.3 %fusion.16 = f32[28,128,128,1]{2,1,3,0:T(8,128)S(1)} fusion(bf16[128,28,16,128]{3,0,2,1:T(8,128)(2,1)} %bitcast.118, bf16[28,16,128,128]{3,2,1,0:T(8,128)(2,1)} %param.11), kind=kOutput, calls=%fused_computation.42 | convolution fusion | flops 1879048192 | bytes 31195136 | tf_op jit(solution)/shard_map/tsnb,snbc->tsc/dot_general | solution.py:30
  96.0 14.6 %broadcast_select_fusion.1 = bf16[448,128,128]{2,1,0:T(8,128)(2,1)} fusion(bf16[448,128,128]{2,1,0:T(8,128)(2,1)} %gather_fusion, pred[448]{0:T(512)(128)(4,1)S(1)} %compare_and_fusion.1), kind=kLoop, calls=%fused_computation.8 | loop fusion | flops 7340032 | bytes 29360576 | tf_op jit(solution)/shard_map/jit(_take)/select_n | solution.py:27
  110.6 10.5 %convert_bitcast_fusion = bf16[16,1,28,128,128]{3,4,0,2,1:T(8,128)(2,1)} fusion(bf16[128,28,16,128]{3,0,2,1:T(8,128)(2,1)} %bitcast.122, f32[28,128,128,1]{2,1,3,0:T(8,128)S(1)} %fusion.16, bf16[128,28,128]{2,0,1:T(8,128)(2,1)S(1)} %copy-done.1, f32[28]{0:T(128)S(1)} %compare_convert_fusion), kind=kOutput, calls=%fused_computation.5 | convolution fusion | flops 1890058240 | bytes 32112752 | tf_op jit(solution)/shard_map/tsnb,tsc->nsbc/dot_general | solution.py:63
  121.0 14.4 %fusion.9 = bf16[128,28,128,1]{2,0,3,1:T(8,128)(2,1)} fusion(f32[28,128,128,1]{2,1,3,0:T(8,128)S(1)} %fusion.16, bf16[128,28,16,128]{3,0,2,1:T(8,128)(2,1)} %bitcast.123, bf16[28,16,128,128]{3,2,1,0:T(8,128)(2,1)} %param.12, bf16[128,28,128]{2,0,1:T(8,128)(2,1)S(1)} %copy-done.1, f32[28]{0:T(128)S(1)} %compare_convert_fusion), kind=kOutput, calls=%fused_computation.25 | convolution fusion | flops 1884553216 | bytes 33030256 | tf_op jit(solution)/shard_map/tsnb,snbc->tsc/dot_general | solution.py:33
  135.4 10.6 %convert_bitcast_fusion.1 = bf16[16,1,28,128,128]{3,4,0,2,1:T(8,128)(2,1)} fusion(bf16[128,28,128,1]{2,0,3,1:T(8,128)(2,1)} %fusion.9, bf16[128,28,16,128]{3,0,2,1:T(8,128)(2,1)} %bitcast.119), kind=kOutput, calls=%fused_computation.6 | convolution fusion | flops 1886388224 | bytes 30277632 | tf_op jit(solution)/shard_map/tsnb,tsc->nsbc/dot_general | solution.py:60
  146.0 20.1 %pad_maximum_fusion = bf16[16,2,28,128,128]{3,4,0,2,1:T(8,128)(2,1)} fusion(bf16[16,1,28,128,128]{3,4,0,2,1:T(8,128)(2,1)} %convert_bitcast_fusion, bf16[16,1,28,128,128]{3,4,0,2,1:T(8,128)(2,1)} %convert_bitcast_fusion.1), kind=kLoop, calls=%fused_computation.4 | loop fusion | flops 14680064 | bytes 58720256 | tf_op jit(solution)/shard_map/stack | solution.py:65
  167.2 14.9 %fusion.17 = f32[28,128,16,128]{3,1,2,0:T(8,128)} fusion(bf16[128,28,128,1]{2,0,3,1:T(8,128)(2,1)S(1)} %copy-done.2, bf16[28,16,128,128]{3,2,1,0:T(8,128)(2,1)} %param.11), kind=kOutput, calls=%fused_computation.43 | convolution fusion | flops 1879048192 | bytes 44957696 | tf_op jit(solution)/shard_map/tsc,snbc->tsnb/dot_general | solution.py:42
  182.3 59.4 %scatter_fusion = f32[128,32,128]{2,0,1:T(8,128)S(1)} fusion(f32[128,32,128]{2,0,1:T(8,128)S(1)} %broadcast_in_dim.8, s32[448]{0:T(512)S(1)} %bitcast.126, f32[448,128,128]{2,1,0:T(8,128)} %bitcast.120), kind=kCustom, calls=%fused_computation.2 | custom fusion | flops 7340032 | bytes 88082176 | tf_op jit(solution)/shard_map/scatter-add | solution.py:47
  241.7 15.4 %fusion.11 = f32[28,128,16,128]{3,1,2,0:T(8,128)} fusion(bf16[28,16,128,128]{3,2,1,0:T(8,128)(2,1)} %param.12, f32[28,128,128,1]{2,1,3,0:T(8,128)} %copy-done, bf16[128,28,128]{2,0,1:T(8,128)(2,1)S(1)} %copy-done.1, f32[28]{0:T(128)S(1)} %compare_convert_fusion), kind=kOutput, calls=%fused_computation.27 | convolution fusion | flops 1882718208 | bytes 46792816 | tf_op jit(solution)/shard_map/tsc,snbc->tsnb/dot_general | solution.py:45
  257.1 59.2 %scatter_fusion.1 = f32[128,32,128]{2,0,1:T(8,128)S(1)} fusion(f32[128,32,128]{2,0,1:T(8,128)S(1)} %scatter_fusion, s32[448]{0:T(512)S(1)} %bitcast.125, f32[448,128,128]{2,1,0:T(8,128)} %bitcast.121), kind=kCustom, calls=%fused_computation.3 | custom fusion | flops 7340032 | bytes 88082176 | tf_op jit(solution)/shard_map/scatter-add | solution.py:50
  316.4 1.3 copy.49
  317.7 3.6 all-to-all-start
  322.6 24.8 %all-to-all-done = bf16[128,4,1024]{0,2,1:T(8,128)(2,1)S(1)} async-done(((bf16[128,4,1024]{0,2,1:T(8,128)(2,1)}), bf16[128,4,1024]{0,2,1:T(8,128)(2,1)S(1)}, u32[]{:S(2)}, u32[]{:S(2)}) %all-to-all-start) | async-done | bytes 1048608 | tf_op jit(solution)/shard_map/all_to_all | solution.py:54
  348.5 307.7 %all-reduce.3.cloned.1.call-done = bf16[16,2,28,128,128]{3,4,0,2,1:T(8,128)(2,1)} async-done(((bf16[16,2,28,128,128]{3,4,0,2,1:T(8,128)(2,1)}), bf16[16,2,28,128,128]{3,4,0,2,1:T(8,128)(2,1)}) %all-reduce.3.cloned.1.call-update) | async-done | bytes 29360144
  656.2 9.4 %dynamic-slice_bitcast_fusion = (bf16[28,4,128,128]{2,3,1,0:T(8,128)(2,1)}, bf16[28,4,128,128]{2,3,1,0:T(8,128)(2,1)}) fusion(bf16[16,2,28,128,128]{3,4,0,2,1:T(8,128)(2,1)} %all-reduce.3.cloned.1.call-done, u32[]{:T(128)S(6)} %multiply.1, u32[]{:T(128)S(6)} %convert.17), kind=kLoop, calls=%fused_computation.9 | loop fusion | bytes 14680072 | tf_op jit(solution)/shard_map/convert_element_type | solution.py:71
  665.6 5.9 copy.53
  671.5 5.9 copy.54
  (31 shorter events, 4.9 us)
Async XLA Ops:
  7.2 33.6 %all-gather.2.cloned.1.call-start = ((), (), s32[]{:S(2)}) async-start(), calls=%async_computation.1 | async-start | bytes 1310720 | tf_op jit(solution)/shard_map/all_gather | solution.py:22
  9.0 647.2 %all-reduce.3.cloned.1.call-start = ((), (), s32[]{:S(2)}) async-start(), calls=%async_computation.2 | async-start | bytes 58720256
  96.0 25.1 %copy-start = (f32[28,128,128,1]{2,1,3,0:T(8,128)}, f32[28,128,128,1]{2,1,3,0:T(8,128)S(1)}, u32[]{:S(2)}) copy-start(f32[28,128,128,1]{2,1,3,0:T(8,128)S(1)} %fusion.16) | copy-start | bytes 5505028
  96.0 14.6 %copy-start.1 = (bf16[128,28,128]{2,0,1:T(8,128)(2,1)S(1)}, bf16[128,28,128]{2,0,1:T(8,128)(2,1)}, u32[]{:S(2)}) copy-start(bf16[128,28,128]{2,0,1:T(8,128)(2,1)} %param.10) | copy-start | bytes 2752516
  166.1 1.2 copy-start.2
  257.1 64.3 %copy-start.3 = (u32[32]{0:T(128)S(1)}, u32[32]{0:T(128)}, u32[]{:S(2)}) copy-start(u32[32]{0:T(128)} %constant.26) | copy-start | bytes 388
  317.7 29.6 %all-to-all-start = ((bf16[128,4,1024]{0,2,1:T(8,128)(2,1)}), bf16[128,4,1024]{0,2,1:T(8,128)(2,1)S(1)}, u32[]{:S(2)}, u32[]{:S(2)}) async-start(bf16[128,4,1024]{0,2,1:T(8,128)(2,1)} %bitcast.24), calls=%async_computation | async-start | bytes 2097152 | tf_op jit(solution)/shard_map/all_to_all | solution.py:54
Sparse Core Ops, SparseCore 0:
  10.1 30.6 all-gather.1
  166.2 489.9 all-reduce.2
where the time goes:
time: 687 us; the launch traced here: 684 us
  waiting for transfers between devices  361 us (53%)
  other arithmetic  171 us (25%)
  matrix products  79 us (11%)
  local copies, waits for them, and re-layouts  55.3 us (8%)
  between operations  14.8 us (2%)
    unnamed x3, waiting for transfers between devices  308 us
    scatter-add x1, other arithmetic, body(): partial_value.at[:, rows_gate.reshape(-1)]  59.4 us
    scatter-add x1, other arithmetic, body(): partial_value.at[:, rows_up.reshape(-1)]  59.2 us
    all_gather x1, waiting for transfers between devices, body(): gathered = lax.all_gather(tokens_in, 'tensor', axis=1, tiled=True)  28.4 us
    all_to_all x1, waiting for transfers between devices, body(): lax.all_to_all(partial_value.astype(jnp.bfloat16), 'tensor', split_axis=1...  24.8 us
    another operation x1, other arithmetic, body(): jnp.stack((part_gate, part_up), axis=1).astype(jnp.bfloat16)  20.1 us
    unnamed x13, local copies, waits for them, and re-layouts  16 us
    dot_general x1, matrix products, body(): jnp.einsum('tsc,snbc->tsnb', up_cot, up_blocks, preferred_element_type=jn...  15.4 us
  transfers between devices with their start and end apart: 3, of which 3 were waited for; matrix products, arithmetic and copies ran while one was open for 23% of the time, Pallas kernels for 0%

commit v1 on v0

v1 whole, which is shorter than its diff:
```python
import functools

import jax
import jax.numpy as jnp
from jax import lax
from jax.experimental import pallas as pl
from jax.experimental.pallas import tpu as pltpu
from jax.sharding import PartitionSpec as P

VMEM_LIMIT = 48 * 1024 * 1024
CHUNKS = 2


def nt(a, b):
    return lax.dot_general(a, b, (((1,), (1,)), ((), ())), preferred_element_type=jnp.float32)


def slot_kernel(first, nonzero, rows_gate, rows_up, x_ref, hid_ref, wg_ref, wu_ref, start_ref, cot_ref, acc_ref):
    step = pl.program_id(0)
    slot = first + step

    @pl.when(step == 0)
    def _():
        acc_ref[...] = start_ref[...]

    block = wg_ref.shape[-1]
    depth = nonzero * block
    picked_gate = jnp.concatenate([x_ref[rows_gate[slot, k]] for k in range(nonzero)], axis=1)
    gate = jnp.dot(picked_gate, wg_ref[0].reshape(depth, block), preferred_element_type=jnp.float32)
    picked_up = jnp.concatenate([x_ref[rows_up[slot, k]] for k in range(nonzero)], axis=1)
    up = jnp.dot(picked_up, wu_ref[0].reshape(depth, block), preferred_element_type=jnp.float32)
    hid = hid_ref[0].astype(jnp.float32)
    p = jax.nn.sigmoid(gate)
    gate_cot = (hid * up * p * (1.0 + gate * (1.0 - p))).astype(jnp.bfloat16)
    up_cot = (hid * gate * p).astype(jnp.bfloat16)
    cot_ref[0, 0] = gate_cot
    cot_ref[0, 1] = up_cot
    for rows, cot, w_ref in ((rows_gate, gate_cot, wg_ref), (rows_up, up_cot, wu_ref)):
        for k in range(0, nonzero, 2):
            pair = nt(cot, w_ref[0, k : k + 2].reshape(2 * block, block))
            acc_ref[rows[slot, k]] += pair[:, :block]
            acc_ref[rows[slot, k + 1]] += pair[:, block:]


def slots_call(first, count, rows_gate, rows_up, x_blocks, hid, wg, wu, start):
    row_blocks, tokens, block = x_blocks.shape
    nonzero = wg.shape[1]
    whole = pl.BlockSpec(x_blocks.shape, lambda i, a, b: (0, 0, 0))
    weight = pl.BlockSpec((1, nonzero, block, block), lambda i, a, b: (first + i, 0, 0, 0))
    flops = count * nonzero * 2 * 2 * 2 * tokens * block * block
    return pl.pallas_call(
        functools.partial(slot_kernel, first, nonzero),
        grid_spec=pltpu.PrefetchScalarGridSpec(
            num_scalar_prefetch=2,
            grid=(count,),
            in_specs=[
                whole,
                pl.BlockSpec((1, tokens, block), lambda i, a, b: (first + i, 0, 0)),
                weight,
                weight,
                whole,
            ],
            out_specs=[
                pl.BlockSpec((1, 2, tokens, block), lambda i, a, b: (i, 0, 0, 0)),
                whole,
            ],
        ),
        out_shape=[
            jax.ShapeDtypeStruct((count, 2, tokens, block), jnp.bfloat16),
            jax.ShapeDtypeStruct(x_blocks.shape, jnp.float32),
        ],
        compiler_params=pltpu.CompilerParams(
            dimension_semantics=("arbitrary",), vmem_limit_bytes=VMEM_LIMIT
        ),
        cost_estimate=pl.CostEstimate(
            flops=flops, bytes_accessed=count * nonzero * 4 * block * block, transcendentals=0
        ),
    )(rows_gate, rows_up, x_blocks, hid, wg, wu, start)


def grad_kernel(first, replicas, rows_gate, rows_up, xt_ref, cot_ref, *rest):
    gg_ref, gu_ref = rest[-2:]
    slot = first + pl.program_id(0)
    own = gg_ref.shape[1]
    per = xt_ref.shape[1]
    block = gg_ref.shape[-1]
    for which, (rows, out_ref) in enumerate(((rows_gate, gg_ref), (rows_up, gu_ref))):
        cot = cot_ref[:, 0, which].reshape(-1, block)
        for k in range(own):
            row = rows[slot, k]
            owner = lax.div(row, per)
            inner = row - owner * per
            lhs = jnp.concatenate(
                [xt_ref[owner * replicas + r, inner] for r in range(replicas)], axis=1
            )
            out_ref[0, k] = jnp.dot(lhs, cot, preferred_element_type=jnp.float32).astype(jnp.bfloat16)


def grads_call(first, count, slot_count, replicas, rows_gate, rows_up, xt, cots, before):
    own = rows_gate.shape[1]
    tokens, block = cots.shape[-2:]
    out = jax.ShapeDtypeStruct((slot_count, own, block, block), jnp.bfloat16)
    out_spec = pl.BlockSpec((1, own, block, block), lambda i, a, b: (first + i, 0, 0, 0))
    extra = () if before is None else before
    return pl.pallas_call(
        functools.partial(grad_kernel, first, replicas),
        grid_spec=pltpu.PrefetchScalarGridSpec(
            num_scalar_prefetch=2,
            grid=(count,),
            in_specs=[
                pl.BlockSpec(xt.shape, lambda i, a, b: (0, 0, 0, 0)),
                pl.BlockSpec((replicas, 1, 2, tokens, block), lambda i, a, b: (0, i, 0, 0, 0)),
            ]
            + [pl.BlockSpec(memory_space=pl.ANY)] * len(extra),
            out_specs=[out_spec, out_spec],
        ),
        out_shape=[out, out],
        input_output_aliases={} if before is None else {4: 0, 5: 1},
        compiler_params=pltpu.CompilerParams(
            dimension_semantics=("arbitrary",), vmem_limit_bytes=VMEM_LIMIT
        ),
        cost_estimate=pl.CostEstimate(
            flops=count * own * 2 * 2 * replicas * tokens * block * block,
            bytes_accessed=count * own * 4 * block * block,
            transcendentals=0,
        ),
    )(rows_gate, rows_up, xt, cots, *extra)


def body(tokens_in, hidden_grad, gate_blocks, up_blocks, gate_rows, up_rows, column_of_slot):
    tokens, local_width = tokens_in.shape
    slot_count, nonzero, block = gate_blocks.shape[:3]
    column_count = gate_rows.shape[0]
    owners = lax.axis_size("tensor")
    replicas = lax.axis_size("dp")
    per = local_width // block
    own = nonzero // replicas
    column_hot = (
        column_of_slot[:, None] == jnp.arange(column_count, dtype=jnp.int32)[None, :]
    ).astype(jnp.int32)
    rows_gate = jnp.sum(column_hot[:, :, None] * gate_rows[None, :, :], axis=1)
    rows_up = jnp.sum(column_hot[:, :, None] * up_rows[None, :, :], axis=1)
    in_use = (column_of_slot < column_count).astype(jnp.bfloat16)

    x_local = tokens_in.reshape(tokens, per, block).transpose(1, 0, 2)
    x_blocks = lax.all_gather(x_local, "tensor", axis=0, tiled=True)
    hid = (hidden_grad * in_use[None, :, None]).transpose(1, 0, 2)
    xt_local = tokens_in.T.reshape(per, block, tokens)
    xt = lax.all_gather(xt_local, ("tensor", "dp"), axis=0, tiled=False)

    index = lax.axis_index("dp")
    own_gate = lax.dynamic_slice_in_dim(rows_gate, index * own, own, axis=1)
    own_up = lax.dynamic_slice_in_dim(rows_up, index * own, own, axis=1)

    chunks = CHUNKS if slot_count % CHUNKS == 0 else 1
    count = slot_count // chunks
    total = jnp.zeros(x_blocks.shape, jnp.float32)
    gathered = []
    for c in range(chunks):
        cots, total = slots_call(
            c * count, count, rows_gate, rows_up, x_blocks, hid, gate_blocks, up_blocks, total
        )
        gathered.append(lax.all_gather(cots, "dp", axis=0, tiled=False))
    arrived = lax.all_to_all(
        total.astype(jnp.bfloat16).reshape(owners, per, tokens, block),
        "tensor",
        split_axis=0,
        concat_axis=0,
        tiled=True,
    )
    tokens_grad = (
        jnp.sum(arrived.astype(jnp.float32), axis=0)
        .astype(jnp.bfloat16)
        .transpose(1, 0, 2)
        .reshape(tokens, local_width)
    )
    grads = None
    for c in range(chunks):
        grads = grads_call(
            c * count, count, slot_count, replicas, own_gate, own_up, xt, gathered[c], grads
        )
    return (tokens_grad, grads[0], grads[1])


def solution(mesh):
    placed = (
        P(("groups", "dp"), "tensor"),
        P(("groups", "dp"), "tensor", None),
        P("tensor", None, None, None),
        P("tensor", None, None, None),
        P(),
        P(),
        P("tensor"),
    )
    return jax.shard_map(
        body,
        mesh=mesh,
        in_specs=placed,
        out_specs=(
            P(("groups", "dp"), "tensor"),
            P("tensor", ("groups", "dp"), None, None),
            P("tensor", ("groups", "dp"), None, None),
        ),
        check_vma=False,
    )
```

time: 687 us -> 205 us (0.30)
  waiting for transfers between devices: 361 us -> 107 us
  other arithmetic: 171 us -> 7.36 us
  matrix products: 79 us -> 0 us
  Pallas kernels: 0 us -> 59.2 us
  local copies, waits for them, and re-layouts: 55.3 us -> 13.4 us
    unnamed x3 -> x4, waiting for transfers between devices: 308 us -> 0.07 us
    scatter-add x2 -> x0, other arithmetic: 119 us -> none  [the longest x1 59.4 us: body(): partial_value.at[:, rows_gate.reshape(-1)]]
    dot_general x6 -> x0, matrix products: 79 us -> none  [the longest x1 15.4 us: body(): jnp.einsum('tsc,snbc->tsnb', up_cot, up_blocks, preferred_element_type=jn...]
    pallas_call x0 -> x4, Pallas kernels: none -> 59.2 us  [the longest x2 36.5 us: slots_call(): pl.pallas_call(functools.partial(slot_kernel, first, nonzero), grid_spec=...]
    all_gather x1 -> x4, waiting for transfers between devices: 28.4 us -> 72.3 us  [the longest x1 27.2 us: body(): xt = lax.all_gather(xt_local, ('tensor', 'dp'), axis=0, tiled=False)]
    select_n x6 -> x0, other arithmetic: 28.4 us -> none  [the longest x2 14.6 us: body(): jnp.take(token_blocks, rows_up.reshape(-1), axis=1)]
    gather x2 -> x0, local copies, waits for them, and re-layouts: 26.4 us -> none  [the longest x1 13.3 us: body(): jnp.take(token_blocks, rows_up.reshape(-1), axis=1)]
    another operation x1 -> x0, other arithmetic: 20.1 us -> none  [body(): jnp.stack((part_gate, part_up), axis=1).astype(jnp.bfloat16)]
  transfers between devices with their start and end apart: 3 -> 5, of which waited for: 3 -> 4; matrix products, arithmetic and copies ran while one was open for 23% -> 5% of each run, Pallas kernels for 0% -> 15%
where the time goes in v1:
time: 205 us; the launch traced here: 204 us
  waiting for transfers between devices  107 us (52%)
  Pallas kernels  59.2 us (29%)
  between operations  13.8 us (7%)
  local copies, waits for them, and re-layouts  13.4 us (7%)
  other arithmetic  7.36 us (4%)
  starting transfers between devices  3.7 us (2%)
    pallas_call x2, Pallas kernels, slots_call(): pl.pallas_call(functools.partial(slot_kernel, first, nonzero), grid_spec=...  36.5 us
    all_to_all x1, waiting for transfers between devices, body(): lax.all_to_all(total.astype(jnp.bfloat16).reshape(owners, per, tokens, bl...  34.3 us
    all_gather x1, waiting for transfers between devices, body(): xt = lax.all_gather(xt_local, ('tensor', 'dp'), axis=0, tiled=False)  27.2 us
    all_gather x1, waiting for transfers between devices, body(): x_blocks = lax.all_gather(x_local, 'tensor', axis=0, tiled=True)  27.1 us
    pallas_call x2, Pallas kernels, grads_call(): pl.pallas_call(functools.partial(grad_kernel, first, replicas), grid_spec...  22.8 us
    all_gather x2, waiting for transfers between devices, body(): gathered.append(lax.all_gather(cots, 'dp', axis=0, tiled=False))  18 us
    unnamed x16, local copies, waits for them, and re-layouts  9.92 us
  transfers between devices with their start and end apart: 5, of which 4 were waited for; matrix products, arithmetic and copies ran while one was open for 5% of the time, Pallas kernels for 15%

profile of v1, /device:TPU:0, one launch (start us, length us, event | category | flops | bytes accessed | tf_op | source)
XLA Modules:
  0.0 204.2 jit_solution(4172044459135736091)
XLA Ops:
  7.2 1.1 copy.32
  8.3 0.9 copy.33
  9.3 0.7 fusion
  10.0 1.7 multiply_reduce_fusion
  11.7 0.7 compare_convert_fusion
  12.4 1.3 multiply_bitcast_fusion.hid_ref
  13.7 27.1 %all-gather.7.cloned.1.call-done.x_ref = bf16[32,128,128]{2,1,0:T(8,128)(2,1)} async-done(((bf16[8,128,128]{2,1,0:T(8,128)(2,1)}), bf16[32,128,128]{2,1,0:T(8,128)(2,1)}) %all-gather.7.cloned.1.call-update) | async-done | bytes 1048592 | tf_op jit(solution)/shard_map/all_gather | solution.py:146
  40.8 1.6 broadcast_in_dim.2.start_ref
  42.4 1.2 copy-done
  43.6 18.1 %shard_map.94 = (bf16[14,2,128,128]{3,2,1,0:T(8,128)(2,1)}, f32[32,128,128]{2,1,0:T(8,128)S(1)}) custom-call(s32[28,16]{1,0:T(8,128)S(1)} %get-tuple-element.26.rows_gate, s32[28,16]{1,0:T(8,128)S(1)} %get-tuple-element.25.rows_up, bf16[32,128,128]{2,1,0:T(8,128)(2,1)S(1)} %copy-done, bf16[28,128,128]{2,1,0:T(8,128)(2,1)S(1)} %multiply_bitcast_fusion.hid_ref, ...), custom_call_target="tpu_custom_call" | custom-call | flops 3758096384 | bytes 14680064 | tf_op jit(solution)/shard_map/pallas_call | solution.py:51
  61.7 1.3 copy-done.4
  63.1 0.8 copy.35
  64.0 18.3 %shard_map.95 = (bf16[14,2,128,128]{3,2,1,0:T(8,128)(2,1)}, f32[32,128,128]{2,1,0:T(8,128)S(1)}) custom-call(s32[28,16]{1,0:T(8,128)S(1)} %get-tuple-element.26.rows_gate, s32[28,16]{1,0:T(8,128)S(1)} %get-tuple-element.25.rows_up, bf16[32,128,128]{2,1,0:T(8,128)(2,1)S(1)} %copy-done.1, bf16[28,128,128]{2,1,0:T(8,128)(2,1)S(1)} %multiply_bitcast_fusion.hid_ref, ...), custom_call_target="tpu_custom_call" | custom-call | flops 3758096384 | bytes 14680064 | tf_op jit(solution)/shard_map/pallas_call | solution.py:51
  82.4 1.3 copy-done.5
  83.7 2.7 %convert_element_type.17 = bf16[32,128,128]{2,1,0:T(8,128)(2,1)} convert(f32[32,128,128]{2,1,0:T(8,128)} %copy-done.5) | non-fusion elementwise | flops 524288 | bytes 3145728 | tf_op jit(solution)/shard_map/convert_element_type | solution.py:165
  86.5 3.5 %all-to-all-start = ((bf16[4,8,128,128]{3,2,1,0:T(8,128)(2,1)}), bf16[4,8,128,128]{3,2,1,0:T(8,128)(2,1)S(1)}, u32[]{:S(2)}, u32[]{:S(2)}) async-start(bf16[4,8,128,128]{3,2,1,0:T(8,128)(2,1)} %bitcast.3), calls=%async_computation | async-start | bytes 2097152 | tf_op jit(solution)/shard_map/all_to_all | solution.py:164
  90.1 34.3 %all-to-all-done = bf16[4,8,128,128]{3,2,1,0:T(8,128)(2,1)S(1)} async-done(((bf16[4,8,128,128]{3,2,1,0:T(8,128)(2,1)}), bf16[4,8,128,128]{3,2,1,0:T(8,128)(2,1)S(1)}, u32[]{:S(2)}, u32[]{:S(2)}) %all-to-all-start) | async-done | bytes 1048608 | tf_op jit(solution)/shard_map/all_to_all | solution.py:164
  124.8 0.9 copy.36
  125.6 27.2 %all-gather.9.cloned.1.call-done.xt_ref = bf16[16,8,128,128]{3,2,1,0:T(8,128)(2,1)} async-done(((bf16[1,8,128,128]{3,2,1,0:T(8,128)(2,1)}), bf16[16,8,128,128]{3,2,1,0:T(8,128)(2,1)}) %all-gather.9.cloned.1.call-update) | async-done | bytes 4194320 | tf_op jit(solution)/shard_map/all_gather | solution.py:149
  152.8 2.0 copy-done.2
  154.8 11.4 %shard_map.96 = (bf16[28,4,128,128]{3,2,1,0:T(8,128)(2,1)}, bf16[28,4,128,128]{3,2,1,0:T(8,128)(2,1)}) custom-call(s32[28,4]{1,0:T(8,128)S(1)} %get-tuple-element.28.rows_gate, s32[28,4]{1,0:T(8,128)S(1)} %get-tuple-element.27.rows_up, bf16[16,8,128,128]{3,2,1,0:T(8,128)(2,1)} %all-gather.9.cloned.1.call-done.xt_ref, bf16[4,14,2,128,128]{4,3,2,1,0:T(8,128)(2,1)S(1)} %bitcast.12), custom_call_target="tpu_custom_call" | custom-call | flops 1879048192 | bytes 3670016 | tf_op jit(solution)/shard_map/pallas_call | solution.py:105
  166.2 18.0 %all-gather.11.cloned.1.call-done = bf16[56,2,128,128]{3,2,1,0:T(8,128)(2,1)} async-done(((bf16[14,2,128,128]{3,2,1,0:T(8,128)(2,1)}), bf16[56,2,128,128]{3,2,1,0:T(8,128)(2,1)}) %all-gather.11.cloned.1.call-update) | async-done | bytes 3670032 | tf_op jit(solution)/shard_map/all_gather | solution.py:163
  184.2 2.0 copy-done.3
  186.3 11.4 %shard_map.97 = (bf16[28,4,128,128]{3,2,1,0:T(8,128)(2,1)}, bf16[28,4,128,128]{3,2,1,0:T(8,128)(2,1)}) custom-call(s32[28,4]{1,0:T(8,128)S(1)} %get-tuple-element.28.rows_gate, s32[28,4]{1,0:T(8,128)S(1)} %get-tuple-element.27.rows_up, bf16[16,8,128,128]{3,2,1,0:T(8,128)(2,1)} %all-gather.9.cloned.1.call-done.xt_ref, ...), custom_call_target="tpu_custom_call", output_to_operand_aliasing={{0}: (4, {}), {1}: (5, {})} | custom-call | flops 1879048192 | bytes 3670016 | tf_op jit(solution)/shard_map/pallas_call | solution.py:105
  (21 shorter events, 0.7 us)
Async XLA Ops:
  7.2 33.6 %all-gather.7.cloned.1.call-start = ((), (), s32[]{:S(2)}) async-start(), calls=%async_computation.1 | async-start | bytes 1310720 | tf_op jit(solution)/shard_map/all_gather | solution.py:146
  9.2 116.4 %all-gather.13.cloned.1.call-start = ((), (), s32[]{:S(2)}) async-start(), calls=%async_computation.4 | async-start | bytes 4587520 | tf_op jit(solution)/shard_map/all_gather | solution.py:163
  42.4 1.2 copy-start
  43.6 19.5 %copy-start.6 = (bf16[128,1024]{1,0:T(8,128)(2,1)S(1)}, bf16[128,1024]{1,0:T(8,128)(2,1)}, u32[]{:S(2)}) copy-start(bf16[128,1024]{1,0:T(8,128)(2,1)} %param.7) | copy-start | bytes 786436
  43.6 20.4 %copy-start.1 = (bf16[32,128,128]{2,1,0:T(8,128)(2,1)S(1)}, bf16[32,128,128]{2,1,0:T(8,128)(2,1)}, u32[]{:S(2)}) copy-start(bf16[32,128,128]{2,1,0:T(8,128)(2,1)} %all-gather.7.cloned.1.call-done.x_ref) | copy-start | bytes 3145732
  61.7 1.3 copy-start.4
  63.1 89.7 %all-gather.9.cloned.1.call-start = ((), (), s32[]{:S(2)}) async-start(), calls=%async_computation.2 | async-start | bytes 4456448 | tf_op jit(solution)/shard_map/all_gather | solution.py:149
  64.0 120.3 %all-gather.11.cloned.1.call-start = ((), (), s32[]{:S(2)}) async-start(), calls=%async_computation.3 | async-start | bytes 4587520 | tf_op jit(solution)/shard_map/all_gather | solution.py:163
  82.4 1.3 copy-start.5
  86.5 37.9 %all-to-all-start = ((bf16[4,8,128,128]{3,2,1,0:T(8,128)(2,1)}), bf16[4,8,128,128]{3,2,1,0:T(8,128)(2,1)S(1)}, u32[]{:S(2)}, u32[]{:S(2)}) async-start(bf16[4,8,128,128]{3,2,1,0:T(8,128)(2,1)} %bitcast.3), calls=%async_computation | async-start | bytes 2097152 | tf_op jit(solution)/shard_map/all_to_all | solution.py:164
  152.8 2.0 copy-start.2
  184.2 2.0 copy-start.3
Sparse Core Ops, SparseCore 0:
  10.1 30.6 all-gather.6
  63.2 30.9 all-gather.12
  96.4 56.3 all-gather.8
  154.2 29.9 all-gather.10

commit v2 on v1

v2 whole, which is shorter than its diff:
```python
import functools

import jax
import jax.numpy as jnp
from jax import lax
from jax.experimental import pallas as pl
from jax.experimental.pallas import tpu as pltpu
from jax.sharding import PartitionSpec as P

VMEM_LIMIT = 48 * 1024 * 1024
MESH = pl.DeviceIdType.MESH


def gather_kernel(owners, x_ref, hid_ref, xall_ref, hall_ref, send_x, recv_x, send_h, recv_h,
                  send_z, recv_z, send_sx, recv_sx, send_sh, recv_sh, local_sem):
    me = lax.axis_index("tensor")
    rep = lax.axis_index("dp")
    sib = rep + 1 - 2 * lax.rem(rep, 2)
    far = lax.rem(rep + 2, 4)
    slots = hid_ref.shape[0]
    half = slots // 2
    has_left, has_right = me > 0, me < owners - 1

    barrier = pltpu.get_barrier_semaphore()
    pl.semaphore_signal(barrier, inc=1, device_id={"dp": sib}, device_id_type=MESH)
    pl.semaphore_signal(barrier, inc=1, device_id={"dp": far}, device_id_type=MESH)

    @pl.when(has_left)
    def _():
        pl.semaphore_signal(barrier, inc=1, device_id={"tensor": me - 1}, device_id_type=MESH)

    @pl.when(has_right)
    def _():
        pl.semaphore_signal(barrier, inc=1, device_id={"tensor": me + 1}, device_id_type=MESH)

    inner = jnp.where(has_left, 1, 0) + jnp.where(has_right, 1, 0)
    pl.semaphore_wait(barrier, 2 + inner)

    def remote(src, dst, send, recv, where):
        return pltpu.make_async_remote_copy(
            src_ref=src, dst_ref=dst, send_sem=send, recv_sem=recv,
            device_id=where, device_id_type=MESH,
        )

    home = (rep, far)
    from_sib = (sib, lax.rem(sib + 2, 4))

    def far_x(d):
        return remote(x_ref, xall_ref.at[me, d], send_x, recv_x, {"dp": far})

    def far_h(d, piece):
        span = pl.ds(piece * half, half)
        return remote(hid_ref.at[span], hall_ref.at[d, span], send_h.at[piece], recv_h.at[piece], {"dp": far})

    def sib_x(cls, z, owner):
        src = x_ref if (cls == 0 and z is me) else xall_ref.at[z, owner[cls]]
        return remote(src, xall_ref.at[z, owner[cls]], send_sx.at[cls, z], recv_sx.at[cls, z], {"dp": sib})

    def sib_h(cls, piece, owner):
        span = pl.ds(piece * half, half)
        src = hid_ref.at[span] if cls == 0 else hall_ref.at[owner[cls], span]
        return remote(src, hall_ref.at[owner[cls], span], send_sh.at[cls, piece], recv_sh.at[cls, piece], {"dp": sib})

    def along(way, cls, hop, z, to):
        src = x_ref if (cls == 0 and hop == 1) else xall_ref.at[z, home[cls]]
        return remote(src, xall_ref.at[z, home[cls]], send_z.at[way, cls, hop - 1], recv_z.at[way, cls, hop - 1], {"tensor": to})

    def out(way, cls, hop, act):
        step = 1 - 2 * way
        z = me - step * (hop - 1)
        to = me + step
        ok = jnp.logical_and(jnp.logical_and(to >= 0, to < owners), jnp.logical_and(z >= 0, z < owners))

        @pl.when(ok)
        def _():
            act(along(way, cls, hop, jnp.clip(z, 0, owners - 1), jnp.clip(to, 0, owners - 1)))

    def arrive(way, cls, hop):
        step = 1 - 2 * way
        z = me - step * hop

        @pl.when(jnp.logical_and(z >= 0, z < owners))
        def _():
            zc = jnp.clip(z, 0, owners - 1)
            frm = jnp.clip(me - step, 0, owners - 1)
            along(way, cls, hop, zc, frm).wait_recv()
            sib_x(cls, zc, home).start()

    own_x = pltpu.make_async_copy(x_ref, xall_ref.at[me, rep], local_sem.at[0])
    own_h = pltpu.make_async_copy(hid_ref, hall_ref.at[rep], local_sem.at[1])

    far_x(rep).start()
    for way in range(2):
        out(way, 0, 1, lambda c: c.start())
    sib_x(0, me, home).start()
    for piece in range(2):
        far_h(rep, piece).start()
    for piece in range(2):
        sib_h(0, piece, home).start()
    own_x.start()
    own_h.start()
    far_x(far).wait_recv()
    for way in range(2):
        out(way, 1, 1, lambda c: c.start())
    sib_x(1, me, home).start()
    for hop in range(1, owners):
        for cls in range(2):
            for way in range(2):
                arrive(way, cls, hop)
                if hop + 1 < owners:
                    out(way, cls, hop + 1, lambda c: c.start())
        if hop == 2 or owners == 2:
            for piece in range(2):
                far_h(far, piece).wait_recv()
                sib_h(1, piece, home).start()

    own_x.wait()
    own_h.wait()
    far_x(rep).wait_send()
    for piece in range(2):
        far_h(rep, piece).wait_send()
    for hop in range(1, owners):
        for cls in range(2):
            for way in range(2):
                out(way, cls, hop, lambda c: c.wait_send())
    for cls in range(2):
        for piece in range(2):
            sib_h(cls, piece, home).wait_send()
            sib_h(cls, piece, from_sib).wait_recv()
        for z in range(owners):
            sib_x(cls, z, home).wait_send()
            sib_x(cls, z, from_sib).wait_recv()


def gather_all(x_local, hid):
    owners = lax.axis_size("tensor")
    replicas = lax.axis_size("dp")
    if replicas != 4 or owners < 2 or owners > 8 or hid.shape[0] % 2:
        x_all = lax.all_gather(lax.all_gather(x_local, "dp", axis=0), "tensor", axis=0)
        return x_all, lax.all_gather(hid, "dp", axis=0)
    dma = pltpu.SemaphoreType.DMA
    hops = owners - 1
    return pl.pallas_call(
        functools.partial(gather_kernel, owners),
        in_specs=[pl.BlockSpec(memory_space=pl.ANY)] * 2,
        out_specs=[pl.BlockSpec(memory_space=pl.ANY)] * 2,
        out_shape=[
            jax.ShapeDtypeStruct((owners, replicas) + x_local.shape, x_local.dtype),
            jax.ShapeDtypeStruct((replicas,) + hid.shape, hid.dtype),
        ],
        scratch_shapes=[
            dma, dma, dma((2,)), dma((2,)),
            dma((2, 2, hops)), dma((2, 2, hops)),
            dma((2, owners)), dma((2, owners)),
            dma((2, 2)), dma((2, 2)), dma((2,)),
        ],
        compiler_params=pltpu.CompilerParams(collective_id=0, has_side_effects=True),
    )(x_local, hid)


def slot_kernel(nonzero, rows_gate, rows_up, where, x_ref, hid_ref, wg_ref, wu_ref, cot_ref, out_ref, acc_ref):
    slot = pl.program_id(0)

    @pl.when(slot == 0)
    def _():
        acc_ref[...] = jnp.zeros_like(acc_ref)

    per = x_ref.shape[2]
    tokens = x_ref.shape[3]
    block = wg_ref.shape[-1]
    depth = nonzero * block
    rep = where[0]

    def product(rows, w_ref):
        parts = []
        for k in range(nonzero):
            row = rows[slot, k]
            owner = lax.div(row, per)
            parts.append(x_ref[owner, :, row - owner * per].reshape(-1, block))
        return jnp.dot(
            jnp.concatenate(parts, axis=1), w_ref[0].reshape(depth, block),
            preferred_element_type=jnp.float32,
        )

    gate = product(rows_gate, wg_ref)
    up = product(rows_up, wu_ref)
    hid = hid_ref[:, 0].reshape(-1, block).astype(jnp.float32)
    p = jax.nn.sigmoid(gate)
    gate_cot = (hid * up * p * (1.0 + gate * (1.0 - p))).astype(jnp.bfloat16)
    up_cot = (hid * gate * p).astype(jnp.bfloat16)
    cot_ref[0, 0] = gate_cot
    cot_ref[0, 1] = up_cot
    mine = pl.ds(pl.multiple_of(rep * tokens, tokens), tokens)
    for which, (rows, w_ref) in enumerate(((rows_gate, wg_ref), (rows_up, wu_ref))):
        cot = cot_ref[0, which, mine, :].T
        back = jnp.dot(w_ref[0].reshape(depth, block), cot, preferred_element_type=jnp.float32)
        for k in range(nonzero):
            acc_ref[rows[slot, k]] += back[k * block : (k + 1) * block]

    @pl.when(slot == pl.num_programs(0) - 1)
    def _():
        for r in range(acc_ref.shape[0]):
            out_ref[r] = acc_ref[r].T.astype(jnp.bfloat16)


def slots_call(rows_gate, rows_up, where, x_all, hid_all, wg, wu):
    owners, replicas, per, tokens, block = x_all.shape
    slot_count, nonzero = wg.shape[:2]
    row_blocks = owners * per
    weight = pl.BlockSpec((1, nonzero, block, block), lambda i, a, b, c: (i, 0, 0, 0))
    return pl.pallas_call(
        functools.partial(slot_kernel, nonzero),
        grid_spec=pltpu.PrefetchScalarGridSpec(
            num_scalar_prefetch=3,
            grid=(slot_count,),
            in_specs=[
                pl.BlockSpec(x_all.shape, lambda i, a, b, c: (0, 0, 0, 0, 0)),
                pl.BlockSpec((replicas, 1, tokens, block), lambda i, a, b, c: (0, i, 0, 0)),
                weight,
                weight,
            ],
            out_specs=[
                pl.BlockSpec((1, 2, replicas * tokens, block), lambda i, a, b, c: (i, 0, 0, 0)),
                pl.BlockSpec((row_blocks, tokens, block), lambda i, a, b, c: (0, 0, 0)),
            ],
            scratch_shapes=[pltpu.VMEM((row_blocks, block, tokens), jnp.float32)],
        ),
        out_shape=[
            jax.ShapeDtypeStruct((slot_count, 2, replicas * tokens, block), jnp.bfloat16),
            jax.ShapeDtypeStruct((row_blocks, tokens, block), jnp.bfloat16),
        ],
        compiler_params=pltpu.CompilerParams(
            dimension_semantics=("arbitrary",), vmem_limit_bytes=VMEM_LIMIT
        ),
        cost_estimate=pl.CostEstimate(
            flops=slot_count * nonzero * 2 * 5 * 2 * tokens * block * block,
            bytes_accessed=slot_count * nonzero * 4 * block * block,
            transcendentals=0,
        ),
    )(rows_gate, rows_up, where, x_all, hid_all, wg, wu)


def grad_kernel(rows_gate, rows_up, x_ref, cot_ref, gg_ref, gu_ref, xt_ref):
    slot = pl.program_id(0)
    owners, _, per, _, block = x_ref.shape
    own = gg_ref.shape[1]

    @pl.when(slot == 0)
    def _():
        for t in range(owners):
            for i in range(per):
                xt_ref[t * per + i] = x_ref[t, :, i].reshape(-1, block).T

    for which, (rows, out_ref) in enumerate(((rows_gate, gg_ref), (rows_up, gu_ref))):
        lhs = jnp.concatenate([xt_ref[rows[slot, k]] for k in range(own)], axis=0)
        both = jnp.dot(lhs, cot_ref[0, which], preferred_element_type=jnp.float32)
        out_ref[0] = both.reshape(own, block, block).astype(jnp.bfloat16)


def grads_call(rows_gate, rows_up, x_all, cots):
    own = rows_gate.shape[1]
    owners, replicas, per, tokens, block = x_all.shape
    slot_count = cots.shape[0]
    out = jax.ShapeDtypeStruct((slot_count, own, block, block), jnp.bfloat16)
    out_spec = pl.BlockSpec((1, own, block, block), lambda i, a, b: (i, 0, 0, 0))
    return pl.pallas_call(
        grad_kernel,
        grid_spec=pltpu.PrefetchScalarGridSpec(
            num_scalar_prefetch=2,
            grid=(slot_count,),
            in_specs=[
                pl.BlockSpec(x_all.shape, lambda i, a, b: (0, 0, 0, 0, 0)),
                pl.BlockSpec((1, 2, replicas * tokens, block), lambda i, a, b: (i, 0, 0, 0)),
            ],
            out_specs=[out_spec, out_spec],
            scratch_shapes=[pltpu.VMEM((owners * per, block, replicas * tokens), jnp.bfloat16)],
        ),
        out_shape=[out, out],
        compiler_params=pltpu.CompilerParams(
            dimension_semantics=("arbitrary",), vmem_limit_bytes=VMEM_LIMIT
        ),
        cost_estimate=pl.CostEstimate(
            flops=slot_count * own * 2 * 2 * replicas * tokens * block * block,
            bytes_accessed=slot_count * own * 4 * block * block,
            transcendentals=0,
        ),
    )(rows_gate, rows_up, x_all, cots)


def body(tokens_in, hidden_grad, gate_blocks, up_blocks, gate_rows, up_rows, column_of_slot):
    tokens, local_width = tokens_in.shape
    slot_count, nonzero, block = gate_blocks.shape[:3]
    column_count = gate_rows.shape[0]
    owners = lax.axis_size("tensor")
    replicas = lax.axis_size("dp")
    per = local_width // block
    own = nonzero // replicas
    column_hot = (
        column_of_slot[:, None] == jnp.arange(column_count, dtype=jnp.int32)[None, :]
    ).astype(jnp.int32)
    rows_gate = jnp.sum(column_hot[:, :, None] * gate_rows[None, :, :], axis=1)
    rows_up = jnp.sum(column_hot[:, :, None] * up_rows[None, :, :], axis=1)
    in_use = (column_of_slot < column_count).astype(jnp.bfloat16)

    x_local = tokens_in.reshape(tokens, per, block).transpose(1, 0, 2)
    hid = (hidden_grad * in_use[None, :, None]).transpose(1, 0, 2)
    x_all, hid_all = gather_all(x_local, hid)

    index = lax.axis_index("dp")
    own_gate = lax.dynamic_slice_in_dim(rows_gate, index * own, own, axis=1)
    own_up = lax.dynamic_slice_in_dim(rows_up, index * own, own, axis=1)

    cots, total = slots_call(
        rows_gate, rows_up, index.reshape(1).astype(jnp.int32), x_all, hid_all, gate_blocks, up_blocks
    )
    arrived = lax.all_to_all(
        total.reshape(owners, per, tokens, block), "tensor", split_axis=0, concat_axis=0, tiled=True
    )
    tokens_grad = (
        jnp.sum(arrived.astype(jnp.float32), axis=0)
        .astype(jnp.bfloat16)
        .transpose(1, 0, 2)
        .reshape(tokens, local_width)
    )
    gate_grad, up_grad = grads_call(own_gate, own_up, x_all, cots)
    return (tokens_grad, gate_grad, up_grad)


def solution(mesh):
    placed = (
        P(("groups", "dp"), "tensor"),
        P(("groups", "dp"), "tensor", None),
        P("tensor", None, None, None),
        P("tensor", None, None, None),
        P(),
        P(),
        P("tensor"),
    )
    return jax.shard_map(
        body,
        mesh=mesh,
        in_specs=placed,
        out_specs=(
            P(("groups", "dp"), "tensor"),
            P("tensor", ("groups", "dp"), None, None),
            P("tensor", ("groups", "dp"), None, None),
        ),
        check_vma=False,
    )
```

time: 205 us -> 143 us (0.70)
  waiting for transfers between devices: 107 us -> 0.01 us
  Pallas kernels: 59.2 us -> 124 us
  between operations: 13.8 us -> 0.67 us
  local copies, waits for them, and re-layouts: 13.4 us -> 7.31 us
    all_gather x4 -> x0, waiting for transfers between devices: 72.3 us -> none  [the longest x1 27.2 us: body(): xt = lax.all_gather(xt_local, ('tensor', 'dp'), axis=0, tiled=False)]
    pallas_call x4 -> x3, Pallas kernels: 59.2 us -> 124 us  [the longest x1 57.2 us: slots_call(): pl.pallas_call(functools.partial(slot_kernel, nonzero), grid_spec=pltpu.P...]
    all_to_all x1, waiting for transfers between devices: 34.3 us -> 0.01 us  [body(): lax.all_to_all(total.reshape(owners, per, tokens, block), 'tensor', split...]
    unnamed x16 -> x6, local copies, waits for them, and re-layouts: 9.92 us -> 6.2 us
    convert_element_type x1 -> x0, other arithmetic: 2.73 us -> none  [body(): total.astype(jnp.bfloat16).reshape(owners, per, tokens, block)]
  transfers between devices with their start and end apart: 5 -> 1, of which waited for: 4 -> 0; matrix products, arithmetic and copies ran while one was open for 5% -> 0% of each run, Pallas kernels for 15% -> 17%
where the time goes in v2:
time: 143 us; the launch traced here: 142 us
  Pallas kernels  124 us (87%)
  local copies, waits for them, and re-layouts  7.31 us (5%)
  other arithmetic  5.56 us (4%)
  starting transfers between devices  3.74 us (3%)
    pallas_call x1, Pallas kernels, slots_call(): pl.pallas_call(functools.partial(slot_kernel, nonzero), grid_spec=pltpu.P...  57.2 us
    pallas_call x1, Pallas kernels, gather_all(): pl.pallas_call(functools.partial(gather_kernel, owners), in_specs=[pl.Blo...  42.7 us
    pallas_call x1, Pallas kernels, grads_call(): pl.pallas_call(grad_kernel, grid_spec=pltpu.PrefetchScalarGridSpec(num_sc...  24.6 us
    unnamed x6, local copies, waits for them, and re-layouts  6.2 us
    all_to_all x1, starting transfers between devices, body(): lax.all_to_all(total.reshape(owners, per, tokens, block), 'tensor', split...  3.74 us
  transfers between devices with their start and end apart: 1, of which 0 were waited for; matrix products, arithmetic and copies ran while one was open for 0% of the time, Pallas kernels for 17%

profile of v2, /device:TPU:0, one launch (start us, length us, event | category | flops | bytes accessed | tf_op | source)
XLA Modules:
  0.0 141.8 jit_solution(5336628590816855114)
XLA Ops:
  0.6 0.7 compare_convert_fusion
  1.3 0.7 fusion
  2.0 1.1 copy.26
  3.1 0.9 copy.27
  4.0 2.2 %multiply_bitcast_fusion.hid_ref = bf16[28,128,128]{2,1,0:T(8,128)(2,1)} fusion(bf16[128,28,128]{2,0,1:T(8,128)(2,1)} %param.8, bf16[28]{0:T(256)(128)(2,1)S(1)} %compare_convert_fusion), kind=kLoop, calls=%fused_computation | loop fusion | flops 458752 | bytes 1835064 | tf_op jit(solution)/shard_map/transpose | solution.py:306
  6.2 42.7 %shard_map.94 = (bf16[4,4,8,128,128]{4,3,2,1,0:T(8,128)(2,1)}, bf16[4,28,128,128]{3,2,1,0:T(8,128)(2,1)}) custom-call(bf16[8,128,128]{2,1,0:T(8,128)(2,1)} %bitcast.11, bf16[28,128,128]{2,1,0:T(8,128)(2,1)} %multiply_bitcast_fusion.hid_ref), custom_call_target="tpu_custom_call" | custom-call | tf_op jit(solution)/shard_map/pallas_call | solution.py:143
  48.9 1.7 %multiply_reduce_fusion = (s32[28,16]{1,0:T(8,128)S(1)}, s32[28,16]{1,0:T(8,128)S(1)}) fusion(s32[112,16]{0,1:T(8,128)} %param.12, s32[28,112]{1,0:T(8,128)S(1)} %fusion, s32[112,16]{0,1:T(8,128)} %param.11), kind=kLoop, calls=%fused_computation.1 | loop fusion | flops 199808 | bytes 30464 | tf_op jit(solution)/shard_map/reduce_sum | solution.py:302
  50.7 0.0 copy-start.1
  50.7 2.0 %copy-done.1 = bf16[4,28,128,128]{3,2,1,0:T(8,128)(2,1)S(1)} copy-done((bf16[4,28,128,128]{3,2,1,0:T(8,128)(2,1)S(1)}, bf16[4,28,128,128]{3,2,1,0:T(8,128)(2,1)}, u32[]{:S(2)}) %copy-start.1) | copy-done | bytes 3670040
  52.7 57.2 %shard_map.95 = (bf16[28,2,512,128]{3,2,1,0:T(8,128)(2,1)}, bf16[32,128,128]{2,1,0:T(8,128)(2,1)}) custom-call(s32[28,16]{1,0:T(8,128)S(1)} %get-tuple-element.22.rows_gate, s32[28,16]{1,0:T(8,128)S(1)} %get-tuple-element.21.rows_up, s32[1]{0:T(128)} %bitcast.where, bf16[4,4,8,128,128]{4,3,2,1,0:T(8,128)(2,1)} %get-tuple-element.9.x_ref, ...), custom_call_target="tpu_custom_call" | custom-call | flops 18790481920 | bytes 29360128 | tf_op jit(solution)/shard_map/pallas_call | solution.py:211
  109.9 3.7 %all-to-all-start = ((bf16[4,8,128,128]{3,2,1,0:T(8,128)(2,1)}), bf16[4,8,128,128]{3,2,1,0:T(8,128)(2,1)S(1)}, u32[]{:S(2)}, u32[]{:S(2)}) async-start(bf16[4,8,128,128]{3,2,1,0:T(8,128)(2,1)} %bitcast.4), calls=%async_computation | async-start | bytes 2097152 | tf_op jit(solution)/shard_map/all_to_all | solution.py:316
  113.7 0.1 constant_dynamic-slice_fusion
  113.8 0.0 copy-start
  113.8 2.2 %copy-done = bf16[4,4,8,128,128]{4,3,2,1,0:T(8,128)(2,1)S(1)} copy-done((bf16[4,4,8,128,128]{4,3,2,1,0:T(8,128)(2,1)S(1)}, bf16[4,4,8,128,128]{4,3,2,1,0:T(8,128)(2,1)}, u32[]{:S(2)}) %copy-start) | copy-done | bytes 4194328
  116.0 24.6 %shard_map.96 = (bf16[28,4,128,128]{3,2,1,0:T(8,128)(2,1)}, bf16[28,4,128,128]{3,2,1,0:T(8,128)(2,1)}) custom-call(s32[28,4]{1,0:T(8,128)S(1)} %get-tuple-element.24.rows_gate, s32[28,4]{1,0:T(8,128)S(1)} %get-tuple-element.23.rows_up, bf16[4,4,8,128,128]{4,3,2,1,0:T(8,128)(2,1)S(1)} %copy-done, bf16[28,2,512,128]{3,2,1,0:T(8,128)(2,1)} %get-tuple-element.12.cot_ref), custom_call_target="tpu_custom_call" | custom-call | flops 3758096384 | bytes 7340032 | tf_op jit(solution)/shard_map/pallas_call | solution.py:266
  140.5 0.0 all-to-all-done
  140.5 0.2 reduce_sum.32
  140.7 0.2 copy.28
  140.9 0.9 copy.29
Async XLA Ops:
  50.7 2.0 %copy-start.1 = (bf16[4,28,128,128]{3,2,1,0:T(8,128)(2,1)S(1)}, bf16[4,28,128,128]{3,2,1,0:T(8,128)(2,1)}, u32[]{:S(2)}) copy-start(bf16[4,28,128,128]{3,2,1,0:T(8,128)(2,1)} %get-tuple-element.10.hid_ref) | copy-start | bytes 11010052
  109.9 30.6 %all-to-all-start = ((bf16[4,8,128,128]{3,2,1,0:T(8,128)(2,1)}), bf16[4,8,128,128]{3,2,1,0:T(8,128)(2,1)S(1)}, u32[]{:S(2)}, u32[]{:S(2)}) async-start(bf16[4,8,128,128]{3,2,1,0:T(8,128)(2,1)} %bitcast.4), calls=%async_computation | async-start | bytes 2097152 | tf_op jit(solution)/shard_map/all_to_all | solution.py:316
  113.8 2.2 %copy-start = (bf16[4,4,8,128,128]{4,3,2,1,0:T(8,128)(2,1)S(1)}, bf16[4,4,8,128,128]{4,3,2,1,0:T(8,128)(2,1)}, u32[]{:S(2)}) copy-start(bf16[4,4,8,128,128]{4,3,2,1,0:T(8,128)(2,1)} %get-tuple-element.9.x_ref) | copy-start | bytes 12582916

commit v3 on v2

--- a/solution.py
+++ b/solution.py
@@ -19,6 +19,8 @@
     far = lax.rem(rep + 2, 4)
     slots = hid_ref.shape[0]
     half = slots // 2
+    mine = lax.rem(rep, 2)
+    theirs = 1 - mine
     has_left, has_right = me > 0, me < owners - 1
 
     barrier = pltpu.get_barrier_semaphore()
@@ -59,7 +61,7 @@
     def sib_h(cls, piece, owner):
         span = pl.ds(piece * half, half)
         src = hid_ref.at[span] if cls == 0 else hall_ref.at[owner[cls], span]
-        return remote(src, hall_ref.at[owner[cls], span], send_sh.at[cls, piece], recv_sh.at[cls, piece], {"dp": sib})
+        return remote(src, hall_ref.at[owner[cls], span], send_sh.at[cls], recv_sh.at[cls], {"dp": sib})
 
     def along(way, cls, hop, z, to):
         src = x_ref if (cls == 0 and hop == 1) else xall_ref.at[z, home[cls]]
@@ -93,10 +95,9 @@
     for way in range(2):
         out(way, 0, 1, lambda c: c.start())
     sib_x(0, me, home).start()
-    for piece in range(2):
-        far_h(rep, piece).start()
-    for piece in range(2):
-        sib_h(0, piece, home).start()
+    far_h(rep, theirs).start()
+    far_h(rep, mine).start()
+    sib_h(0, theirs, home).start()
     own_x.start()
     own_h.start()
     far_x(far).wait_recv()
@@ -110,13 +111,13 @@
                 if hop + 1 < owners:
                     out(way, cls, hop + 1, lambda c: c.start())
         if hop == 2 or owners == 2:
-            for piece in range(2):
-                far_h(far, piece).wait_recv()
-                sib_h(1, piece, home).start()
+            far_h(far, theirs).wait_recv()
+            sib_h(1, theirs, home).start()
 
     own_x.wait()
     own_h.wait()
     far_x(rep).wait_send()
+    far_h(far, mine).wait_recv()
     for piece in range(2):
         far_h(rep, piece).wait_send()
     for hop in range(1, owners):
@@ -124,9 +125,8 @@
             for way in range(2):
                 out(way, cls, hop, lambda c: c.wait_send())
     for cls in range(2):
-        for piece in range(2):
-            sib_h(cls, piece, home).wait_send()
-            sib_h(cls, piece, from_sib).wait_recv()
+        sib_h(cls, theirs, home).wait_send()
+        sib_h(cls, mine, from_sib).wait_recv()
         for z in range(owners):
             sib_x(cls, z, home).wait_send()
             sib_x(cls, z, from_sib).wait_recv()
@@ -152,16 +152,17 @@
             dma, dma, dma((2,)), dma((2,)),
             dma((2, 2, hops)), dma((2, 2, hops)),
             dma((2, owners)), dma((2, owners)),
-            dma((2, 2)), dma((2, 2)), dma((2,)),
+            dma((2,)), dma((2,)), dma((2,)),
         ],
         compiler_params=pltpu.CompilerParams(collective_id=0, has_side_effects=True),
     )(x_local, hid)
 
 
-def slot_kernel(nonzero, rows_gate, rows_up, where, x_ref, hid_ref, wg_ref, wu_ref, cot_ref, out_ref, acc_ref):
-    slot = pl.program_id(0)
-
-    @pl.when(slot == 0)
+def slot_kernel(nonzero, rows_gate, rows_up, where, x_ref, hid_ref, wg_ref, wu_ref, cot_ref, keep_ref, give_ref, acc_ref):
+    step = pl.program_id(0)
+    slot = where[1] + step
+
+    @pl.when(step == 0)
     def _():
         acc_ref[...] = jnp.zeros_like(acc_ref)
 
@@ -190,24 +191,29 @@
     up_cot = (hid * gate * p).astype(jnp.bfloat16)
     cot_ref[0, 0] = gate_cot
     cot_ref[0, 1] = up_cot
-    mine = pl.ds(pl.multiple_of(rep * tokens, tokens), tokens)
+    core = lax.rem(rep, 2)
+    pair = pl.ds(pl.multiple_of((rep - core) * tokens, 2 * tokens), 2 * tokens)
     for which, (rows, w_ref) in enumerate(((rows_gate, wg_ref), (rows_up, wu_ref))):
-        cot = cot_ref[0, which, mine, :].T
+        cot = cot_ref[0, which, pair, :].T
         back = jnp.dot(w_ref[0].reshape(depth, block), cot, preferred_element_type=jnp.float32)
         for k in range(nonzero):
             acc_ref[rows[slot, k]] += back[k * block : (k + 1) * block]
 
-    @pl.when(slot == pl.num_programs(0) - 1)
-    def _():
+    @pl.when(step == pl.num_programs(0) - 1)
+    def _():
+        own = pl.ds(pl.multiple_of(core * tokens, tokens), tokens)
+        other = pl.ds(pl.multiple_of((1 - core) * tokens, tokens), tokens)
         for r in range(acc_ref.shape[0]):
-            out_ref[r] = acc_ref[r].T.astype(jnp.bfloat16)
+            keep_ref[r] = acc_ref[r, :, own].T
+            give_ref[r] = acc_ref[r, :, other].T.astype(jnp.bfloat16)
 
 
 def slots_call(rows_gate, rows_up, where, x_all, hid_all, wg, wu):
     owners, replicas, per, tokens, block = x_all.shape
-    slot_count, nonzero = wg.shape[:2]
+    slot_count, nonzero = wg.shape[0] // 2, wg.shape[1]
     row_blocks = owners * per
-    weight = pl.BlockSpec((1, nonzero, block, block), lambda i, a, b, c: (i, 0, 0, 0))
+    weight = pl.BlockSpec((1, nonzero, block, block), lambda i, a, b, c: (c[1] + i, 0, 0, 0))
+    grad_spec = pl.BlockSpec((row_blocks, tokens, block), lambda i, a, b, c: (0, 0, 0))
     return pl.pallas_call(
         functools.partial(slot_kernel, nonzero),
         grid_spec=pltpu.PrefetchScalarGridSpec(
@@ -215,37 +221,41 @@
             grid=(slot_count,),
             in_specs=[
                 pl.BlockSpec(x_all.shape, lambda i, a, b, c: (0, 0, 0, 0, 0)),
-                pl.BlockSpec((replicas, 1, tokens, block), lambda i, a, b, c: (0, i, 0, 0)),
+                pl.BlockSpec((replicas, 1, tokens, block), lambda i, a, b, c: (0, c[1] + i, 0, 0)),
                 weight,
                 weight,
             ],
             out_specs=[
                 pl.BlockSpec((1, 2, replicas * tokens, block), lambda i, a, b, c: (i, 0, 0, 0)),
-                pl.BlockSpec((row_blocks, tokens, block), lambda i, a, b, c: (0, 0, 0)),
+                grad_spec,
+                grad_spec,
             ],
-            scratch_shapes=[pltpu.VMEM((row_blocks, block, tokens), jnp.float32)],
+            scratch_shapes=[pltpu.VMEM((row_blocks, block, 2 * tokens), jnp.float32)],
         ),
         out_shape=[
             jax.ShapeDtypeStruct((slot_count, 2, replicas * tokens, block), jnp.bfloat16),
+            jax.ShapeDtypeStruct((row_blocks, tokens, block), jnp.float32),
             jax.ShapeDtypeStruct((row_blocks, tokens, block), jnp.bfloat16),
         ],
         compiler_params=pltpu.CompilerParams(
             dimension_semantics=("arbitrary",), vmem_limit_bytes=VMEM_LIMIT
         ),
         cost_estimate=pl.CostEstimate(
-            flops=slot_count * nonzero * 2 * 5 * 2 * tokens * block * block,
+            flops=slot_count * nonzero * 2 * 6 * 2 * tokens * block * block,
             bytes_accessed=slot_count * nonzero * 4 * block * block,
             transcendentals=0,
         ),
     )(rows_gate, rows_up, where, x_all, hid_all, wg, wu)
 
 
-def grad_kernel(rows_gate, rows_up, x_ref, cot_ref, gg_ref, gu_ref, xt_ref):
-    slot = pl.program_id(0)
+def grad_kernel(rows_gate, rows_up, where, x_ref, cot_ref, *rest):
+    gg_ref, gu_ref, xt_ref = rest[-3:]
+    step = pl.program_id(0)
+    slot = where[0] + step
     owners, _, per, _, block = x_ref.shape
     own = gg_ref.shape[1]
 
-    @pl.when(slot == 0)
+    @pl.when(step == 0)
     def _():
         for t in range(owners):
             for i in range(per):
@@ -257,34 +267,36 @@
         out_ref[0] = both.reshape(own, block, block).astype(jnp.bfloat16)
 
 
-def grads_call(rows_gate, rows_up, x_all, cots):
-    own = rows_gate.shape[1]
+def grads_call(rows_gate, rows_up, where, x_all, cots, before):
+    slot_count, own = rows_gate.shape
     owners, replicas, per, tokens, block = x_all.shape
-    slot_count = cots.shape[0]
+    count = cots.shape[0]
     out = jax.ShapeDtypeStruct((slot_count, own, block, block), jnp.bfloat16)
-    out_spec = pl.BlockSpec((1, own, block, block), lambda i, a, b: (i, 0, 0, 0))
+    out_spec = pl.BlockSpec((1, own, block, block), lambda i, a, b, c: (c[0] + i, 0, 0, 0))
     return pl.pallas_call(
         grad_kernel,
         grid_spec=pltpu.PrefetchScalarGridSpec(
-            num_scalar_prefetch=2,
-            grid=(slot_count,),
+            num_scalar_prefetch=3,
+            grid=(count,),
             in_specs=[
-                pl.BlockSpec(x_all.shape, lambda i, a, b: (0, 0, 0, 0, 0)),
-                pl.BlockSpec((1, 2, replicas * tokens, block), lambda i, a, b: (i, 0, 0, 0)),
-            ],
+                pl.BlockSpec(x_all.shape, lambda i, a, b, c: (0, 0, 0, 0, 0)),
+                pl.BlockSpec((1, 2, replicas * tokens, block), lambda i, a, b, c: (i, 0, 0, 0)),
+            ]
+            + [pl.BlockSpec(memory_space=pl.ANY)] * len(before),
             out_specs=[out_spec, out_spec],
             scratch_shapes=[pltpu.VMEM((owners * per, block, replicas * tokens), jnp.bfloat16)],
         ),
         out_shape=[out, out],
+        input_output_aliases={5: 0, 6: 1} if before else {},
         compiler_params=pltpu.CompilerParams(
             dimension_semantics=("arbitrary",), vmem_limit_bytes=VMEM_LIMIT
         ),
         cost_estimate=pl.CostEstimate(
-            flops=slot_count * own * 2 * 2 * replicas * tokens * block * block,
-            bytes_accessed=slot_count * own * 4 * block * block,
+            flops=count * own * 2 * 2 * replicas * tokens * block * block,
+            bytes_accessed=count * own * 4 * block * block,
             transcendentals=0,
         ),
-    )(rows_gate, rows_up, x_all, cots)
+    )(rows_gate, rows_up, where, x_all, cots, *before)
 
 
 def body(tokens_in, hidden_grad, gate_blocks, up_blocks, gate_rows, up_rows, column_of_slot):
@@ -310,9 +322,19 @@
     own_gate = lax.dynamic_slice_in_dim(rows_gate, index * own, own, axis=1)
     own_up = lax.dynamic_slice_in_dim(rows_up, index * own, own, axis=1)
 
-    cots, total = slots_call(
-        rows_gate, rows_up, index.reshape(1).astype(jnp.int32), x_all, hid_all, gate_blocks, up_blocks
-    )
+    half = slot_count // 2
+    core = lax.rem(index, 2)
+    first = (core * half).reshape(1).astype(jnp.int32)
+    second = half - first
+    where = jnp.stack([index.astype(jnp.int32), first[0]])
+    swap = [(i, i + 1 - 2 * (i % 2)) for i in range(replicas)]
+    cots, keep, give = slots_call(
+        rows_gate, rows_up, where, x_all, hid_all, gate_blocks, up_blocks
+    )
+    got = lax.ppermute(give, "dp", swap)
+    total = (keep + got.astype(jnp.float32)).astype(jnp.bfloat16)
+    total, cots = lax.optimization_barrier((total, cots))
+    sib_cots = lax.ppermute(cots, "dp", swap)
     arrived = lax.all_to_all(
         total.reshape(owners, per, tokens, block), "tensor", split_axis=0, concat_axis=0, tiled=True
     )
@@ -322,7 +344,8 @@
         .transpose(1, 0, 2)
         .reshape(tokens, local_width)
     )
-    gate_grad, up_grad = grads_call(own_gate, own_up, x_all, cots)
+    grads = grads_call(own_gate, own_up, first, x_all, cots, ())
+    gate_grad, up_grad = grads_call(own_gate, own_up, second, x_all, sib_cots, grads)
     return (tokens_grad, gate_grad, up_grad)
 
 

time: 143 us -> 138 us (0.965)
  Pallas kernels: 124 us -> 110 us
  waiting for transfers between devices: 0.01 us -> 13 us
  local copies, waits for them, and re-layouts: 7.31 us -> 3.09 us
    pallas_call x1, Pallas kernels: 57.2 us -> 37 us  [slots_call(): pl.pallas_call(functools.partial(slot_kernel, nonzero), grid_spec=pltpu.P...]
    all_to_all x1, waiting for transfers between devices: 0.01 us -> 10.7 us  [body(): lax.all_to_all(total.reshape(owners, per, tokens, block), 'tensor', split...]
    pallas_call x1 -> x2, Pallas kernels: 24.6 us -> 30.7 us  [grads_call(): pl.pallas_call(grad_kernel, grid_spec=pltpu.PrefetchScalarGridSpec(num_sc...]
    unnamed x6, local copies, waits for them, and re-layouts: 6.2 us -> 1.98 us
    ppermute x0 -> x2, waiting for transfers between devices: none -> 2.3 us  [the longest x1 2.29 us: body(): got = lax.ppermute(give, 'dp', swap)]
  transfers between devices with their start and end apart: 1 -> 3, of which waited for: 0 -> 2; matrix products, arithmetic and copies ran while one was open for 0% -> 1% of each run, Pallas kernels for 17% -> 11%
where the time goes in v3:
time: 138 us
  Pallas kernels  110 us (80%)
  waiting for transfers between devices  13 us (9%)
  other arithmetic  6.2 us (4%)
  starting transfers between devices  4.46 us (3%)
  local copies, waits for them, and re-layouts  3.09 us (2%)
    pallas_call x1, Pallas kernels, gather_all(): pl.pallas_call(functools.partial(gather_kernel, owners), in_specs=[pl.Blo...  42.6 us
    pallas_call x1, Pallas kernels, slots_call(): pl.pallas_call(functools.partial(slot_kernel, nonzero), grid_spec=pltpu.P...  37 us
    pallas_call x2, Pallas kernels, grads_call(): pl.pallas_call(grad_kernel, grid_spec=pltpu.PrefetchScalarGridSpec(num_sc...  30.7 us
    all_to_all x1, waiting for transfers between devices, body(): lax.all_to_all(total.reshape(owners, per, tokens, block), 'tensor', split...  10.7 us
    all_to_all x1, starting transfers between devices, body(): lax.all_to_all(total.reshape(owners, per, tokens, block), 'tensor', split...  3.73 us
  transfers between devices with their start and end apart: 3, of which 2 were waited for; matrix products, arithmetic and copies ran while one was open for 1% of the time, Pallas kernels for 11%

profile of v3, /device:TPU:0, one launch (start us, length us, event | category | flops | bytes accessed | tf_op | source)
XLA Modules:
  0.0 137.7 jit_solution(893465343725555837)
XLA Ops:
  0.6 0.0 copy-start
  0.6 0.0 copy-start.1
  0.7 0.7 compare_convert_fusion
  1.3 0.7 fusion
  2.0 1.1 copy.28
  3.2 0.9 copy.29
  4.0 0.1 pad_add_fusion.where
  4.1 2.2 %multiply_bitcast_fusion.hid_ref = bf16[28,128,128]{2,1,0:T(8,128)(2,1)} fusion(bf16[128,28,128]{2,0,1:T(8,128)(2,1)} %param.8, bf16[28]{0:T(256)(128)(2,1)S(1)} %compare_convert_fusion), kind=kLoop, calls=%fused_computation.1 | loop fusion | flops 458752 | bytes 1835064 | tf_op jit(solution)/shard_map/transpose | solution.py:318
  6.3 42.6 %shard_map.94 = (bf16[4,4,8,128,128]{4,3,2,1,0:T(8,128)(2,1)}, bf16[4,28,128,128]{3,2,1,0:T(8,128)(2,1)}) custom-call(bf16[8,128,128]{2,1,0:T(8,128)(2,1)} %bitcast.12, bf16[28,128,128]{2,1,0:T(8,128)(2,1)} %multiply_bitcast_fusion.hid_ref), custom_call_target="tpu_custom_call" | custom-call | tf_op jit(solution)/shard_map/pallas_call | solution.py:143
  49.0 1.0 multiply_reduce_fusion
  50.0 37.0 %shard_map.95 = (bf16[14,2,512,128]{3,2,1,0:T(8,128)(2,1)}, f32[32,128,128]{2,1,0:T(8,128)S(1)}, bf16[32,128,128]{2,1,0:T(8,128)(2,1)S(1)}) custom-call(s32[28,16]{1,0:T(8,128)S(1)} %get-tuple-element.32.rows_gate, s32[28,16]{1,0:T(8,128)S(1)} %get-tuple-element.31.rows_up, s32[2]{0:T(128)S(1)} %pad_add_fusion.where, ...), custom_call_target="tpu_custom_call" | custom-call | flops 11274289152 | bytes 14680064 | tf_op jit(solution)/shard_map/pallas_call | solution.py:217
  87.0 0.4 collective-permute-start
  87.4 2.3 %collective-permute-done = bf16[32,128,128]{2,1,0:T(8,128)(2,1)S(1)} collective-permute-done((bf16[32,128,128]{2,1,0:T(8,128)(2,1)S(1)}, bf16[32,128,128]{2,1,0:T(8,128)(2,1)S(1)}, u32[]{:S(2)}, u32[]{:S(2)}) %collective-permute-start) | collective-permute-done | bytes 1048608 | tf_op jit(solution)/shard_map/ppermute | solution.py:334
  89.6 1.3 add_convert_fusion
  90.9 0.4 collective-permute-start.1
  91.3 3.7 %all-to-all-start = ((bf16[4,8,128,128]{3,2,1,0:T(8,128)(2,1)}), bf16[4,8,128,128]{3,2,1,0:T(8,128)(2,1)S(1)}, u32[]{:S(2)}, u32[]{:S(2)}) async-start(bf16[4,8,128,128]{3,2,1,0:T(8,128)(2,1)} %bitcast.5), calls=%async_computation | async-start | bytes 2097152 | tf_op jit(solution)/shard_map/all_to_all | solution.py:338
  95.0 0.1 constant_dynamic-slice_fusion
  95.1 15.3 %shard_map.96 = (bf16[28,4,128,128]{3,2,1,0:T(8,128)(2,1)}, bf16[28,4,128,128]{3,2,1,0:T(8,128)(2,1)}) custom-call(s32[28,4]{1,0:T(8,128)S(1)} %get-tuple-element.34.rows_gate, s32[28,4]{1,0:T(8,128)S(1)} %get-tuple-element.33.rows_up, s32[1]{0:T(128)} %bitcast.1.where, bf16[4,4,8,128,128]{4,3,2,1,0:T(8,128)(2,1)} %get-tuple-element.14.x_ref, ...), custom_call_target="tpu_custom_call" | custom-call | flops 1879048192 | bytes 3670016 | tf_op jit(solution)/shard_map/pallas_call | solution.py:276
  110.4 10.7 %all-to-all-done = bf16[4,8,128,128]{3,2,1,0:T(8,128)(2,1)S(1)} async-done(((bf16[4,8,128,128]{3,2,1,0:T(8,128)(2,1)}), bf16[4,8,128,128]{3,2,1,0:T(8,128)(2,1)S(1)}, u32[]{:S(2)}, u32[]{:S(2)}) %all-to-all-start) | async-done | bytes 1048608 | tf_op jit(solution)/shard_map/all_to_all | solution.py:338
  121.1 0.2 reduce_sum.32
  121.3 0.2 copy.30
  121.5 0.9 copy.31
  122.3 0.0 collective-permute-done.1.cot_ref
  122.3 15.3 %shard_map.97 = (bf16[28,4,128,128]{3,2,1,0:T(8,128)(2,1)}, bf16[28,4,128,128]{3,2,1,0:T(8,128)(2,1)}) custom-call(s32[28,4]{1,0:T(8,128)S(1)} %get-tuple-element.34.rows_gate, s32[28,4]{1,0:T(8,128)S(1)} %get-tuple-element.33.rows_up, s32[1]{0:T(128)S(6)} %sub.3.where, ...), custom_call_target="tpu_custom_call", output_to_operand_aliasing={{0}: (5, {}), {1}: (6, {})} | custom-call | flops 1879048192 | bytes 3670016 | tf_op jit(solution)/shard_map/pallas_call | solution.py:276
  (2 shorter events, 0.0 us)
Async XLA Ops:
  0.6 48.4 %copy-start = (s32[112,16]{0,1:T(8,128)S(1)}, s32[112,16]{0,1:T(8,128)}, u32[]{:S(2)}) copy-start(s32[112,16]{0,1:T(8,128)} %param.12) | copy-start | bytes 21508
  0.6 48.4 %copy-start.1 = (s32[112,16]{0,1:T(8,128)S(1)}, s32[112,16]{0,1:T(8,128)}, u32[]{:S(2)}) copy-start(s32[112,16]{0,1:T(8,128)} %param.11) | copy-start | bytes 21508
  87.0 2.7 %collective-permute-start = (bf16[32,128,128]{2,1,0:T(8,128)(2,1)S(1)}, bf16[32,128,128]{2,1,0:T(8,128)(2,1)S(1)}, u32[]{:S(2)}, u32[]{:S(2)}) collective-permute-start(bf16[32,128,128]{2,1,0:T(8,128)(2,1)S(1)} %get-tuple-element.17), channel_id=1, source_target_pairs={{0,1},{1,0},{2,3},{3,2},{4,5},{5,4},{6,7},{7,6},{8,9},{9,8},{10,11... | collective-permute-start | bytes 3145736 | tf_op jit(solution)/shard_map/ppermute | solution.py:334
  90.9 31.4 %collective-permute-start.1 = (bf16[14,2,512,128]{3,2,1,0:T(8,128)(2,1)}, bf16[14,2,512,128]{3,2,1,0:T(8,128)(2,1)}, u32[]{:S(2)}, u32[]{:S(2)}) collective-permute-start(bf16[14,2,512,128]{3,2,1,0:T(8,128)(2,1)} %get-tuple-element.20.cot_ref), channel_id=1, source_target_pairs={{0,1},{1,0},{2,3},{3,2},{4,5},{5,4},{6,7},{7,6},{8,9},{9,8},{10,11... | collective-permute-start | bytes 11010056 | tf_op jit(solution)/shard_map/ppermute | solution.py:337
  91.3 29.8 %all-to-all-start = ((bf16[4,8,128,128]{3,2,1,0:T(8,128)(2,1)}), bf16[4,8,128,128]{3,2,1,0:T(8,128)(2,1)S(1)}, u32[]{:S(2)}, u32[]{:S(2)}) async-start(bf16[4,8,128,128]{3,2,1,0:T(8,128)(2,1)} %bitcast.5), calls=%async_computation | async-start | bytes 2097152 | tf_op jit(solution)/shard_map/all_to_all | solution.py:338

commit v4 on v3

--- a/solution.py
+++ b/solution.py
@@ -95,8 +95,6 @@
     for way in range(2):
         out(way, 0, 1, lambda c: c.start())
     sib_x(0, me, home).start()
-    far_h(rep, theirs).start()
-    far_h(rep, mine).start()
     sib_h(0, theirs, home).start()
     own_x.start()
     own_h.start()
@@ -104,6 +102,8 @@
     for way in range(2):
         out(way, 1, 1, lambda c: c.start())
     sib_x(1, me, home).start()
+    far_h(rep, theirs).start()
+    far_h(rep, mine).start()
     for hop in range(1, owners):
         for cls in range(2):
             for way in range(2):
@@ -166,9 +166,9 @@
     def _():
         acc_ref[...] = jnp.zeros_like(acc_ref)
 
-    per = x_ref.shape[2]
-    tokens = x_ref.shape[3]
     block = wg_ref.shape[-1]
+    tokens = x_ref.shape[2]
+    per = x_ref.shape[3] // block
     depth = nonzero * block
     rep = where[0]
 
@@ -177,7 +177,8 @@
         for k in range(nonzero):
             row = rows[slot, k]
             owner = lax.div(row, per)
-            parts.append(x_ref[owner, :, row - owner * per].reshape(-1, block))
+            lanes = pl.ds(pl.multiple_of((row - owner * per) * block, block), block)
+            parts.append(x_ref[owner, :, :, lanes].reshape(-1, block))
         return jnp.dot(
             jnp.concatenate(parts, axis=1), w_ref[0].reshape(depth, block),
             preferred_element_type=jnp.float32,
@@ -204,23 +205,25 @@
         own = pl.ds(pl.multiple_of(core * tokens, tokens), tokens)
         other = pl.ds(pl.multiple_of((1 - core) * tokens, tokens), tokens)
         for r in range(acc_ref.shape[0]):
-            keep_ref[r] = acc_ref[r, :, own].T
-            give_ref[r] = acc_ref[r, :, other].T.astype(jnp.bfloat16)
+            lanes = pl.ds((r % per) * block, block)
+            keep_ref[r // per, :, lanes] = acc_ref[r, :, own].T
+            give_ref[r // per, :, lanes] = acc_ref[r, :, other].T.astype(jnp.bfloat16)
 
 
 def slots_call(rows_gate, rows_up, where, x_all, hid_all, wg, wu):
-    owners, replicas, per, tokens, block = x_all.shape
+    owners, replicas, tokens, width = x_all.shape
+    block = wg.shape[-1]
     slot_count, nonzero = wg.shape[0] // 2, wg.shape[1]
-    row_blocks = owners * per
+    row_blocks = owners * width // block
     weight = pl.BlockSpec((1, nonzero, block, block), lambda i, a, b, c: (c[1] + i, 0, 0, 0))
-    grad_spec = pl.BlockSpec((row_blocks, tokens, block), lambda i, a, b, c: (0, 0, 0))
+    grad_spec = pl.BlockSpec((owners, tokens, width), lambda i, a, b, c: (0, 0, 0))
     return pl.pallas_call(
         functools.partial(slot_kernel, nonzero),
         grid_spec=pltpu.PrefetchScalarGridSpec(
             num_scalar_prefetch=3,
             grid=(slot_count,),
             in_specs=[
-                pl.BlockSpec(x_all.shape, lambda i, a, b, c: (0, 0, 0, 0, 0)),
+                pl.BlockSpec(x_all.shape, lambda i, a, b, c: (0, 0, 0, 0)),
                 pl.BlockSpec((replicas, 1, tokens, block), lambda i, a, b, c: (0, c[1] + i, 0, 0)),
                 weight,
                 weight,
@@ -234,8 +237,8 @@
         ),
         out_shape=[
             jax.ShapeDtypeStruct((slot_count, 2, replicas * tokens, block), jnp.bfloat16),
-            jax.ShapeDtypeStruct((row_blocks, tokens, block), jnp.float32),
-            jax.ShapeDtypeStruct((row_blocks, tokens, block), jnp.bfloat16),
+            jax.ShapeDtypeStruct((owners, tokens, width), jnp.float32),
+            jax.ShapeDtypeStruct((owners, tokens, width), jnp.bfloat16),
         ],
         compiler_params=pltpu.CompilerParams(
             dimension_semantics=("arbitrary",), vmem_limit_bytes=VMEM_LIMIT
@@ -249,17 +252,21 @@
 
 
 def grad_kernel(rows_gate, rows_up, where, x_ref, cot_ref, *rest):
-    gg_ref, gu_ref, xt_ref = rest[-3:]
+    later = len(rest) > 3
+    gg_ref, gu_ref = rest[2:4] if later else rest[:2]
+    xt_ref = x_ref if later else rest[2]
     step = pl.program_id(0)
     slot = where[0] + step
-    owners, _, per, _, block = x_ref.shape
-    own = gg_ref.shape[1]
-
-    @pl.when(step == 0)
-    def _():
-        for t in range(owners):
-            for i in range(per):
-                xt_ref[t * per + i] = x_ref[t, :, i].reshape(-1, block).T
+    own, block = gg_ref.shape[1], gg_ref.shape[-1]
+
+    if not later:
+
+        @pl.when(step == 0)
+        def _():
+            per = x_ref.shape[3] // block
+            for r in range(xt_ref.shape[0]):
+                lanes = pl.ds((r % per) * block, block)
+                xt_ref[r] = x_ref[r // per, :, :, lanes].reshape(-1, block).T
 
     for which, (rows, out_ref) in enumerate(((rows_gate, gg_ref), (rows_up, gu_ref))):
         lhs = jnp.concatenate([xt_ref[rows[slot, k]] for k in range(own)], axis=0)
@@ -267,45 +274,45 @@
         out_ref[0] = both.reshape(own, block, block).astype(jnp.bfloat16)
 
 
-def grads_call(rows_gate, rows_up, where, x_all, cots, before):
+def grads_call(rows_gate, rows_up, where, x, cots, before):
     slot_count, own = rows_gate.shape
-    owners, replicas, per, tokens, block = x_all.shape
-    count = cots.shape[0]
+    count, _, tokens, block = cots.shape
     out = jax.ShapeDtypeStruct((slot_count, own, block, block), jnp.bfloat16)
     out_spec = pl.BlockSpec((1, own, block, block), lambda i, a, b, c: (c[0] + i, 0, 0, 0))
+    out_shape, out_specs = [out, out], [out_spec, out_spec]
+    if not before:
+        row_blocks = x.shape[0] * x.shape[3] // block
+        out_shape.append(jax.ShapeDtypeStruct((row_blocks, block, tokens), jnp.bfloat16))
+        out_specs.append(pl.BlockSpec((row_blocks, block, tokens), lambda i, a, b, c: (0, 0, 0)))
     return pl.pallas_call(
         grad_kernel,
         grid_spec=pltpu.PrefetchScalarGridSpec(
             num_scalar_prefetch=3,
             grid=(count,),
             in_specs=[
-                pl.BlockSpec(x_all.shape, lambda i, a, b, c: (0, 0, 0, 0, 0)),
-                pl.BlockSpec((1, 2, replicas * tokens, block), lambda i, a, b, c: (i, 0, 0, 0)),
+                pl.BlockSpec(x.shape, lambda i, a, b, c: (0,) * x.ndim),
+                pl.BlockSpec((1, 2, tokens, block), lambda i, a, b, c: (i, 0, 0, 0)),
             ]
             + [pl.BlockSpec(memory_space=pl.ANY)] * len(before),
-            out_specs=[out_spec, out_spec],
-            scratch_shapes=[pltpu.VMEM((owners * per, block, replicas * tokens), jnp.bfloat16)],
-        ),
-        out_shape=[out, out],
+            out_specs=out_specs,
+        ),
+        out_shape=out_shape,
         input_output_aliases={5: 0, 6: 1} if before else {},
         compiler_params=pltpu.CompilerParams(
             dimension_semantics=("arbitrary",), vmem_limit_bytes=VMEM_LIMIT
         ),
         cost_estimate=pl.CostEstimate(
-            flops=count * own * 2 * 2 * replicas * tokens * block * block,
-            bytes_accessed=count * own * 4 * block * block,
+            flops=count * own * 2 * 2 * block * block,
+            bytes_accessed=count * own * 4 * block,
             transcendentals=0,
         ),
-    )(rows_gate, rows_up, where, x_all, cots, *before)
+    )(rows_gate, rows_up, where, x, cots, *before)
 
 
 def body(tokens_in, hidden_grad, gate_blocks, up_blocks, gate_rows, up_rows, column_of_slot):
-    tokens, local_width = tokens_in.shape
-    slot_count, nonzero, block = gate_blocks.shape[:3]
+    slot_count, nonzero = gate_blocks.shape[:2]
     column_count = gate_rows.shape[0]
-    owners = lax.axis_size("tensor")
     replicas = lax.axis_size("dp")
-    per = local_width // block
     own = nonzero // replicas
     column_hot = (
         column_of_slot[:, None] == jnp.arange(column_count, dtype=jnp.int32)[None, :]
@@ -314,9 +321,8 @@
     rows_up = jnp.sum(column_hot[:, :, None] * up_rows[None, :, :], axis=1)
     in_use = (column_of_slot < column_count).astype(jnp.bfloat16)
 
-    x_local = tokens_in.reshape(tokens, per, block).transpose(1, 0, 2)
     hid = (hidden_grad * in_use[None, :, None]).transpose(1, 0, 2)
-    x_all, hid_all = gather_all(x_local, hid)
+    x_all, hid_all = gather_all(tokens_in, hid)
 
     index = lax.axis_index("dp")
     own_gate = lax.dynamic_slice_in_dim(rows_gate, index * own, own, axis=1)
@@ -336,16 +342,11 @@
     total, cots = lax.optimization_barrier((total, cots))
     sib_cots = lax.ppermute(cots, "dp", swap)
     arrived = lax.all_to_all(
-        total.reshape(owners, per, tokens, block), "tensor", split_axis=0, concat_axis=0, tiled=True
+        total, "tensor", split_axis=0, concat_axis=0, tiled=True
     )
-    tokens_grad = (
-        jnp.sum(arrived.astype(jnp.float32), axis=0)
-        .astype(jnp.bfloat16)
-        .transpose(1, 0, 2)
-        .reshape(tokens, local_width)
-    )
-    grads = grads_call(own_gate, own_up, first, x_all, cots, ())
-    gate_grad, up_grad = grads_call(own_gate, own_up, second, x_all, sib_cots, grads)
+    tokens_grad = jnp.sum(arrived.astype(jnp.float32), axis=0).astype(jnp.bfloat16)
+    gate_grad, up_grad, x_turned = grads_call(own_gate, own_up, first, x_all, cots, ())
+    gate_grad, up_grad = grads_call(own_gate, own_up, second, x_turned, sib_cots, (gate_grad, up_grad))
     return (tokens_grad, gate_grad, up_grad)
 
 

time: 138 us -> 136 us (0.986)
  local copies, waits for them, and re-layouts: 3.09 us -> 0.07 us
  other arithmetic: 6.2 us -> 7.71 us
    unnamed x6 -> x0, local copies, waits for them, and re-layouts: 1.98 us -> none
  transfers between devices with their start and end apart: 3 -> 3, of which waited for: 2 -> 2; matrix products, arithmetic and copies ran while one was open for 1% -> 1% of each run, Pallas kernels for 11% -> 12%
where the time goes in v4:
time: 136 us
  Pallas kernels  111 us (82%)
  waiting for transfers between devices  11.9 us (9%)
  other arithmetic  7.71 us (6%)
  starting transfers between devices  4.44 us (3%)
    pallas_call x1, Pallas kernels, gather_all(): pl.pallas_call(functools.partial(gather_kernel, owners), in_specs=[pl.Blo...  42.6 us
    pallas_call x1, Pallas kernels, slots_call(): pl.pallas_call(functools.partial(slot_kernel, nonzero), grid_spec=pltpu.P...  37.6 us
    pallas_call x2, Pallas kernels, grads_call(): pl.pallas_call(grad_kernel, grid_spec=pltpu.PrefetchScalarGridSpec(num_sc...  30.6 us
    all_to_all x1, waiting for transfers between devices, body(): lax.all_to_all(total, 'tensor', split_axis=0, concat_axis=0, tiled=True)  9.6 us
    all_to_all x1, starting transfers between devices, body(): lax.all_to_all(total, 'tensor', split_axis=0, concat_axis=0, tiled=True)  3.66 us
  transfers between devices with their start and end apart: 3, of which 2 were waited for; matrix products, arithmetic and copies ran while one was open for 1% of the time, Pallas kernels for 12%

profile of v4, /device:TPU:0, one launch (start us, length us, event | category | flops | bytes accessed | tf_op | source)
XLA Modules:
  0.0 135.7 jit_solution(13486669351862468341)
XLA Ops:
  0.6 0.7 fusion
  1.4 0.7 compare_convert_fusion
  2.0 0.1 pad_add_fusion.where
  2.1 2.2 %multiply_bitcast_fusion.hid_ref = bf16[28,128,128]{2,1,0:T(8,128)(2,1)} fusion(bf16[128,28,128]{2,0,1:T(8,128)(2,1)} %param.8, bf16[28]{0:T(256)(128)(2,1)S(1)} %compare_convert_fusion), kind=kLoop, calls=%fused_computation.1 | loop fusion | flops 458752 | bytes 1835064 | tf_op jit(solution)/shard_map/transpose | solution.py:324
  4.3 42.6 %shard_map.94 = (bf16[4,4,128,1024]{3,2,1,0:T(8,128)(2,1)}, bf16[4,28,128,128]{3,2,1,0:T(8,128)(2,1)}) custom-call(bf16[128,1024]{1,0:T(8,128)(2,1)} %x_ref.1, bf16[28,128,128]{2,1,0:T(8,128)(2,1)} %multiply_bitcast_fusion.hid_ref), custom_call_target="tpu_custom_call" | custom-call | tf_op jit(solution)/shard_map/pallas_call | solution.py:143
  47.0 1.7 %multiply_reduce_fusion = (s32[28,16]{1,0:T(8,128)S(1)}, s32[28,16]{1,0:T(8,128)S(1)}) fusion(s32[112,16]{0,1:T(8,128)} %param.12, s32[28,112]{1,0:T(8,128)S(1)} %fusion, s32[112,16]{0,1:T(8,128)} %param.11), kind=kLoop, calls=%fused_computation.2 | loop fusion | flops 199808 | bytes 30464 | tf_op jit(solution)/shard_map/reduce_sum | solution.py:321
  48.7 37.6 %shard_map.95 = (bf16[14,2,512,128]{3,2,1,0:T(8,128)(2,1)}, f32[4,128,1024]{2,1,0:T(8,128)S(1)}, bf16[4,128,1024]{2,1,0:T(8,128)(2,1)S(1)}) custom-call(s32[28,16]{1,0:T(8,128)S(1)} %get-tuple-element.28.rows_gate, s32[28,16]{1,0:T(8,128)S(1)} %get-tuple-element.27.rows_up, s32[2]{0:T(128)S(1)} %pad_add_fusion.where, ...), custom_call_target="tpu_custom_call" | custom-call | flops 11274289152 | bytes 14680064 | tf_op jit(solution)/shard_map/pallas_call | solution.py:220
  86.3 0.4 collective-permute-start
  86.7 2.3 %collective-permute-done = bf16[4,128,1024]{2,1,0:T(8,128)(2,1)S(1)} collective-permute-done((bf16[4,128,1024]{2,1,0:T(8,128)(2,1)S(1)}, bf16[4,128,1024]{2,1,0:T(8,128)(2,1)S(1)}, u32[]{:S(2)}, u32[]{:S(2)}) %collective-permute-start) | collective-permute-done | bytes 1048608 | tf_op jit(solution)/shard_map/ppermute | solution.py:340
  89.0 1.4 add_convert_fusion
  90.4 0.4 collective-permute-start.1
  90.8 3.7 %all-to-all-start = ((bf16[4,128,1024]{2,1,0:T(8,128)(2,1)}), bf16[4,128,1024]{2,1,0:T(8,128)(2,1)S(1)}, u32[]{:S(2)}, u32[]{:S(2)}) async-start(bf16[4,128,1024]{2,1,0:T(8,128)(2,1)} %add_convert_fusion), calls=%async_computation | async-start | bytes 2097152 | tf_op jit(solution)/shard_map/all_to_all | solution.py:344
  94.4 0.1 constant_dynamic-slice_fusion
  94.5 16.5 %shard_map.96 = (bf16[28,4,128,128]{3,2,1,0:T(8,128)(2,1)}, bf16[28,4,128,128]{3,2,1,0:T(8,128)(2,1)}, bf16[32,128,512]{2,1,0:T(8,128)(2,1)}) custom-call(s32[28,4]{1,0:T(8,128)S(1)} %get-tuple-element.30.rows_gate, s32[28,4]{1,0:T(8,128)S(1)} %get-tuple-element.29.rows_up, s32[1]{0:T(128)} %bitcast.1.where, ...), custom_call_target="tpu_custom_call" | custom-call | flops 3670016 | bytes 28672 | tf_op jit(solution)/shard_map/pallas_call | solution.py:287
  111.0 9.6 %all-to-all-done = bf16[4,128,1024]{2,1,0:T(8,128)(2,1)S(1)} async-done(((bf16[4,128,1024]{2,1,0:T(8,128)(2,1)}), bf16[4,128,1024]{2,1,0:T(8,128)(2,1)S(1)}, u32[]{:S(2)}, u32[]{:S(2)}) %all-to-all-start) | async-done | bytes 1048608 | tf_op jit(solution)/shard_map/all_to_all | solution.py:344
  120.6 0.9 reduce_sum.32
  121.5 0.0 collective-permute-done.1.cot_ref
  121.5 14.2 %shard_map.97 = (bf16[28,4,128,128]{3,2,1,0:T(8,128)(2,1)}, bf16[28,4,128,128]{3,2,1,0:T(8,128)(2,1)}) custom-call(s32[28,4]{1,0:T(8,128)S(1)} %get-tuple-element.30.rows_gate, s32[28,4]{1,0:T(8,128)S(1)} %get-tuple-element.29.rows_up, s32[1]{0:T(128)S(6)} %sub.3.where, ...), custom_call_target="tpu_custom_call", output_to_operand_aliasing={{0}: (5, {}), {1}: (6, {})} | custom-call | flops 3670016 | bytes 28672 | tf_op jit(solution)/shard_map/pallas_call | solution.py:287
Async XLA Ops:
  86.3 2.7 %collective-permute-start = (bf16[4,128,1024]{2,1,0:T(8,128)(2,1)S(1)}, bf16[4,128,1024]{2,1,0:T(8,128)(2,1)S(1)}, u32[]{:S(2)}, u32[]{:S(2)}) collective-permute-start(bf16[4,128,1024]{2,1,0:T(8,128)(2,1)S(1)} %get-tuple-element.18), channel_id=1, source_target_pairs={{0,1},{1,0},{2,3},{3,2},{4,5},{5,4},{6,7},{7,6},{8,9},{9,8},{10,11... | collective-permute-start | bytes 3145736 | tf_op jit(solution)/shard_map/ppermute | solution.py:340
  90.4 31.1 %collective-permute-start.1 = (bf16[14,2,512,128]{3,2,1,0:T(8,128)(2,1)}, bf16[14,2,512,128]{3,2,1,0:T(8,128)(2,1)}, u32[]{:S(2)}, u32[]{:S(2)}) collective-permute-start(bf16[14,2,512,128]{3,2,1,0:T(8,128)(2,1)} %get-tuple-element.21.cot_ref), channel_id=1, source_target_pairs={{0,1},{1,0},{2,3},{3,2},{4,5},{5,4},{6,7},{7,6},{8,9},{9,8},{10,11... | collective-permute-start | bytes 11010056 | tf_op jit(solution)/shard_map/ppermute | solution.py:343
  90.8 29.8 %all-to-all-start = ((bf16[4,128,1024]{2,1,0:T(8,128)(2,1)}), bf16[4,128,1024]{2,1,0:T(8,128)(2,1)S(1)}, u32[]{:S(2)}, u32[]{:S(2)}) async-start(bf16[4,128,1024]{2,1,0:T(8,128)(2,1)} %add_convert_fusion), calls=%async_computation | async-start | bytes 2097152 | tf_op jit(solution)/shard_map/all_to_all | solution.py:344

commit v5 on v4

--- a/solution.py
+++ b/solution.py
@@ -251,62 +251,73 @@
     )(rows_gate, rows_up, where, x_all, hid_all, wg, wu)
 
 
-def grad_kernel(rows_gate, rows_up, where, x_ref, cot_ref, *rest):
-    later = len(rest) > 3
-    gg_ref, gu_ref = rest[2:4] if later else rest[:2]
-    xt_ref = x_ref if later else rest[2]
+def grad_slot(step, where, half):
+    late = step >= half
+    return jnp.where(late, half - where[0] + step - half, where[0] + step)
+
+
+def grad_kernel(half, rows_gate, rows_up, where, x_ref, cot_ref, sib_ref, gg_ref, gu_ref, xt_ref):
     step = pl.program_id(0)
-    slot = where[0] + step
+    slot = grad_slot(step, where, half)
     own, block = gg_ref.shape[1], gg_ref.shape[-1]
 
-    if not later:
-
-        @pl.when(step == 0)
-        def _():
-            per = x_ref.shape[3] // block
-            for r in range(xt_ref.shape[0]):
-                lanes = pl.ds((r % per) * block, block)
-                xt_ref[r] = x_ref[r // per, :, :, lanes].reshape(-1, block).T
-
-    for which, (rows, out_ref) in enumerate(((rows_gate, gg_ref), (rows_up, gu_ref))):
-        lhs = jnp.concatenate([xt_ref[rows[slot, k]] for k in range(own)], axis=0)
-        both = jnp.dot(lhs, cot_ref[0, which], preferred_element_type=jnp.float32)
-        out_ref[0] = both.reshape(own, block, block).astype(jnp.bfloat16)
-
-
-def grads_call(rows_gate, rows_up, where, x, cots, before):
+    @pl.when(step == 0)
+    def _():
+        per = x_ref.shape[3] // block
+        for r in range(xt_ref.shape[0]):
+            lanes = pl.ds((r % per) * block, block)
+            xt_ref[r] = x_ref[r // per, :, :, lanes].reshape(-1, block).T
+
+    def work(source):
+        for which, (rows, out_ref) in enumerate(((rows_gate, gg_ref), (rows_up, gu_ref))):
+            lhs = jnp.concatenate([xt_ref[rows[slot, k]] for k in range(own)], axis=0)
+            both = jnp.dot(lhs, source[0, which], preferred_element_type=jnp.float32)
+            out_ref[0] = both.reshape(own, block, block).astype(jnp.bfloat16)
+
+    @pl.when(step < half)
+    def _():
+        work(cot_ref)
+
+    @pl.when(step >= half)
+    def _():
+        work(sib_ref)
+
+
+def grads_call(rows_gate, rows_up, where, x_all, cots, sib_cots):
     slot_count, own = rows_gate.shape
-    count, _, tokens, block = cots.shape
+    half, _, tokens, block = cots.shape
+    row_blocks = x_all.shape[0] * x_all.shape[3] // block
     out = jax.ShapeDtypeStruct((slot_count, own, block, block), jnp.bfloat16)
-    out_spec = pl.BlockSpec((1, own, block, block), lambda i, a, b, c: (c[0] + i, 0, 0, 0))
-    out_shape, out_specs = [out, out], [out_spec, out_spec]
-    if not before:
-        row_blocks = x.shape[0] * x.shape[3] // block
-        out_shape.append(jax.ShapeDtypeStruct((row_blocks, block, tokens), jnp.bfloat16))
-        out_specs.append(pl.BlockSpec((row_blocks, block, tokens), lambda i, a, b, c: (0, 0, 0)))
+    out_spec = pl.BlockSpec(
+        (1, own, block, block), lambda i, a, b, c: (grad_slot(i, c, half), 0, 0, 0)
+    )
     return pl.pallas_call(
-        grad_kernel,
+        functools.partial(grad_kernel, half),
         grid_spec=pltpu.PrefetchScalarGridSpec(
             num_scalar_prefetch=3,
-            grid=(count,),
+            grid=(slot_count,),
             in_specs=[
-                pl.BlockSpec(x.shape, lambda i, a, b, c: (0,) * x.ndim),
-                pl.BlockSpec((1, 2, tokens, block), lambda i, a, b, c: (i, 0, 0, 0)),
-            ]
-            + [pl.BlockSpec(memory_space=pl.ANY)] * len(before),
-            out_specs=out_specs,
-        ),
-        out_shape=out_shape,
-        input_output_aliases={5: 0, 6: 1} if before else {},
+                pl.BlockSpec(x_all.shape, lambda i, a, b, c: (0, 0, 0, 0)),
+                pl.BlockSpec(
+                    (1, 2, tokens, block), lambda i, a, b, c: (jnp.minimum(i, half - 1), 0, 0, 0)
+                ),
+                pl.BlockSpec(
+                    (1, 2, tokens, block), lambda i, a, b, c: (jnp.maximum(i - half, 0), 0, 0, 0)
+                ),
+            ],
+            out_specs=[out_spec, out_spec],
+            scratch_shapes=[pltpu.VMEM((row_blocks, block, tokens), jnp.bfloat16)],
+        ),
+        out_shape=[out, out],
         compiler_params=pltpu.CompilerParams(
             dimension_semantics=("arbitrary",), vmem_limit_bytes=VMEM_LIMIT
         ),
         cost_estimate=pl.CostEstimate(
-            flops=count * own * 2 * 2 * block * block,
-            bytes_accessed=count * own * 4 * block,
+            flops=slot_count * own * 2 * 2 * tokens * block * block,
+            bytes_accessed=slot_count * own * 4 * block * block,
             transcendentals=0,
         ),
-    )(rows_gate, rows_up, where, x, cots, *before)
+    )(rows_gate, rows_up, where, x_all, cots, sib_cots)
 
 
 def body(tokens_in, hidden_grad, gate_blocks, up_blocks, gate_rows, up_rows, column_of_slot):
@@ -331,7 +342,6 @@
     half = slot_count // 2
     core = lax.rem(index, 2)
     first = (core * half).reshape(1).astype(jnp.int32)
-    second = half - first
     where = jnp.stack([index.astype(jnp.int32), first[0]])
     swap = [(i, i + 1 - 2 * (i % 2)) for i in range(replicas)]
     cots, keep, give = slots_call(
@@ -339,14 +349,12 @@
     )
     got = lax.ppermute(give, "dp", swap)
     total = (keep + got.astype(jnp.float32)).astype(jnp.bfloat16)
-    total, cots = lax.optimization_barrier((total, cots))
     sib_cots = lax.ppermute(cots, "dp", swap)
     arrived = lax.all_to_all(
         total, "tensor", split_axis=0, concat_axis=0, tiled=True
     )
     tokens_grad = jnp.sum(arrived.astype(jnp.float32), axis=0).astype(jnp.bfloat16)
-    gate_grad, up_grad, x_turned = grads_call(own_gate, own_up, first, x_all, cots, ())
-    gate_grad, up_grad = grads_call(own_gate, own_up, second, x_turned, sib_cots, (gate_grad, up_grad))
+    gate_grad, up_grad = grads_call(own_gate, own_up, first, x_all, cots, sib_cots)
     return (tokens_grad, gate_grad, up_grad)
 
 

time: 136 us -> 152 us (1.12)
  waiting for transfers between devices: 11.9 us -> 33.1 us
  Pallas kernels: 111 us -> 104 us
  local copies, waits for them, and re-layouts: 0.07 us -> 2.11 us
    all_to_all x1, waiting for transfers between devices: 9.6 us -> 26 us  [body(): lax.all_to_all(total, 'tensor', split_axis=0, concat_axis=0, tiled=True)]
    pallas_call x2 -> x1, Pallas kernels: 30.6 us -> 23.7 us  [grads_call(): pl.pallas_call(functools.partial(grad_kernel, half), grid_spec=pltpu.Pref...]
    ppermute x1, waiting for transfers between devices: 2.29 us -> 7.16 us  [body(): got = lax.ppermute(give, 'dp', swap)]
    unnamed x0 -> x2, local copies, waits for them, and re-layouts: none -> 2.04 us
  transfers between devices with their start and end apart: 3 -> 3, of which waited for: 2 -> 2; matrix products, arithmetic and copies ran while one was open for 1% -> 2% of each run, Pallas kernels for 12% -> 0%
where the time goes in v5:
time: 152 us
  Pallas kernels  104 us (68%)
  waiting for transfers between devices  33.1 us (22%)
  other arithmetic  7.7 us (5%)
  starting transfers between devices  4.29 us (3%)
  local copies, waits for them, and re-layouts  2.11 us (1%)
    pallas_call x1, Pallas kernels, gather_all(): pl.pallas_call(functools.partial(gather_kernel, owners), in_specs=[pl.Blo...  42.6 us
    pallas_call x1, Pallas kernels, slots_call(): pl.pallas_call(functools.partial(slot_kernel, nonzero), grid_spec=pltpu.P...  37.6 us
    all_to_all x1, waiting for transfers between devices, body(): lax.all_to_all(total, 'tensor', split_axis=0, concat_axis=0, tiled=True)  26 us
    pallas_call x1, Pallas kernels, grads_call(): pl.pallas_call(functools.partial(grad_kernel, half), grid_spec=pltpu.Pref...  23.7 us
    ppermute x1, waiting for transfers between devices, body(): got = lax.ppermute(give, 'dp', swap)  7.16 us
    all_to_all x1, starting transfers between devices, body(): lax.all_to_all(total, 'tensor', split_axis=0, concat_axis=0, tiled=True)  3.78 us
  transfers between devices with their start and end apart: 3, of which 2 were waited for; matrix products, arithmetic and copies ran while one was open for 2% of the time, Pallas kernels for 0%

profile of v5, /device:TPU:0, one launch (start us, length us, event | category | flops | bytes accessed | tf_op | source)
XLA Modules:
  0.0 151.8 jit_solution(17737469048653749436)
XLA Ops:
  0.6 0.7 compare_convert_fusion
  1.3 0.7 fusion
  2.0 0.1 pad_add_fusion.where
  2.1 2.2 %multiply_bitcast_fusion.hid_ref = bf16[28,128,128]{2,1,0:T(8,128)(2,1)} fusion(bf16[128,28,128]{2,0,1:T(8,128)(2,1)} %param.8, bf16[28]{0:T(256)(128)(2,1)S(1)} %compare_convert_fusion), kind=kLoop, calls=%fused_computation.1 | loop fusion | flops 458752 | bytes 1835064 | tf_op jit(solution)/shard_map/transpose | solution.py:335
  4.3 42.6 %shard_map.94 = (bf16[4,4,128,1024]{3,2,1,0:T(8,128)(2,1)}, bf16[4,28,128,128]{3,2,1,0:T(8,128)(2,1)}) custom-call(bf16[128,1024]{1,0:T(8,128)(2,1)} %x_ref.1, bf16[28,128,128]{2,1,0:T(8,128)(2,1)} %multiply_bitcast_fusion.hid_ref), custom_call_target="tpu_custom_call" | custom-call | tf_op jit(solution)/shard_map/pallas_call | solution.py:143
  47.0 1.7 %multiply_reduce_fusion = (s32[28,16]{1,0:T(8,128)S(1)}, s32[28,16]{1,0:T(8,128)S(1)}) fusion(s32[112,16]{0,1:T(8,128)} %param.12, s32[28,112]{1,0:T(8,128)S(1)} %fusion, s32[112,16]{0,1:T(8,128)} %param.11), kind=kLoop, calls=%fused_computation.2 | loop fusion | flops 199808 | bytes 30464 | tf_op jit(solution)/shard_map/reduce_sum | solution.py:332
  48.7 37.6 %shard_map.95 = (bf16[14,2,512,128]{3,2,1,0:T(8,128)(2,1)}, f32[4,128,1024]{2,1,0:T(8,128)S(1)}, bf16[4,128,1024]{2,1,0:T(8,128)(2,1)S(1)}) custom-call(s32[28,16]{1,0:T(8,128)S(1)} %get-tuple-element.18.rows_gate, s32[28,16]{1,0:T(8,128)S(1)} %get-tuple-element.17.rows_up, s32[2]{0:T(128)S(1)} %pad_add_fusion.where, ...), custom_call_target="tpu_custom_call" | custom-call | flops 11274289152 | bytes 14680064 | tf_op jit(solution)/shard_map/pallas_call | solution.py:220
  86.4 0.4 collective-permute-start.1
  86.7 0.2 collective-permute-start
  86.9 7.2 %collective-permute-done = bf16[4,128,1024]{2,1,0:T(8,128)(2,1)S(1)} collective-permute-done((bf16[4,128,1024]{2,1,0:T(8,128)(2,1)S(1)}, bf16[4,128,1024]{2,1,0:T(8,128)(2,1)S(1)}, u32[]{:S(2)}, u32[]{:S(2)}) %collective-permute-start) | collective-permute-done | bytes 1048608 | tf_op jit(solution)/shard_map/ppermute | solution.py:350
  94.0 1.3 add_convert_fusion
  95.4 3.8 %all-to-all-start = ((bf16[4,128,1024]{2,1,0:T(8,128)(2,1)}), bf16[4,128,1024]{2,1,0:T(8,128)(2,1)S(1)}, u32[]{:S(2)}, u32[]{:S(2)}) async-start(bf16[4,128,1024]{2,1,0:T(8,128)(2,1)} %add_convert_fusion), calls=%async_computation | async-start | bytes 2097152 | tf_op jit(solution)/shard_map/all_to_all | solution.py:353
  99.1 0.1 constant_dynamic-slice_fusion
  99.2 26.0 %all-to-all-done = bf16[4,128,1024]{2,1,0:T(8,128)(2,1)S(1)} async-done(((bf16[4,128,1024]{2,1,0:T(8,128)(2,1)}), bf16[4,128,1024]{2,1,0:T(8,128)(2,1)S(1)}, u32[]{:S(2)}, u32[]{:S(2)}) %all-to-all-start) | async-done | bytes 1048608 | tf_op jit(solution)/shard_map/all_to_all | solution.py:353
  125.2 0.9 reduce_sum.32
  126.1 0.0 collective-permute-done.1.sib_ref
  126.1 0.0 copy-start
  126.1 2.0 %copy-done = bf16[14,2,512,128]{3,2,1,0:T(8,128)(2,1)S(1)} copy-done((bf16[14,2,512,128]{3,2,1,0:T(8,128)(2,1)S(1)}, bf16[14,2,512,128]{3,2,1,0:T(8,128)(2,1)}, u32[]{:S(2)}) %copy-start) | copy-done | bytes 3670040
  128.1 23.7 %shard_map.96 = (bf16[28,4,128,128]{3,2,1,0:T(8,128)(2,1)}, bf16[28,4,128,128]{3,2,1,0:T(8,128)(2,1)}) custom-call(s32[28,4]{1,0:T(8,128)S(1)} %get-tuple-element.20.rows_gate, s32[28,4]{1,0:T(8,128)S(1)} %get-tuple-element.19.rows_up, s32[1]{0:T(128)} %bitcast.1.where, bf16[4,4,128,1024]{3,2,1,0:T(8,128)(2,1)} %get-tuple-element.10.x_ref, ...), custom_call_target="tpu_custom_call" | custom-call | flops 3758096384 | bytes 7340032 | tf_op jit(solution)/shard_map/pallas_call | solution.py:294
Async XLA Ops:
  86.4 39.8 %collective-permute-start.1 = (bf16[14,2,512,128]{3,2,1,0:T(8,128)(2,1)}, bf16[14,2,512,128]{3,2,1,0:T(8,128)(2,1)}, u32[]{:S(2)}, u32[]{:S(2)}) collective-permute-start(bf16[14,2,512,128]{3,2,1,0:T(8,128)(2,1)} %get-tuple-element.14.cot_ref), channel_id=1, source_target_pairs={{0,1},{1,0},{2,3},{3,2},{4,5},{5,4},{6,7},{7,6},{8,9},{9,8},{10,11... | collective-permute-start | bytes 11010056 | tf_op jit(solution)/shard_map/ppermute | solution.py:352
  86.7 7.3 %collective-permute-start = (bf16[4,128,1024]{2,1,0:T(8,128)(2,1)S(1)}, bf16[4,128,1024]{2,1,0:T(8,128)(2,1)S(1)}, u32[]{:S(2)}, u32[]{:S(2)}) collective-permute-start(bf16[4,128,1024]{2,1,0:T(8,128)(2,1)S(1)} %get-tuple-element.13), channel_id=1, source_target_pairs={{0,1},{1,0},{2,3},{3,2},{4,5},{5,4},{6,7},{7,6},{8,9},{9,8},{10,11... | collective-permute-start | bytes 3145736 | tf_op jit(solution)/shard_map/ppermute | solution.py:350
  95.4 29.8 %all-to-all-start = ((bf16[4,128,1024]{2,1,0:T(8,128)(2,1)}), bf16[4,128,1024]{2,1,0:T(8,128)(2,1)S(1)}, u32[]{:S(2)}, u32[]{:S(2)}) async-start(bf16[4,128,1024]{2,1,0:T(8,128)(2,1)} %add_convert_fusion), calls=%async_computation | async-start | bytes 2097152 | tf_op jit(solution)/shard_map/all_to_all | solution.py:353
  126.1 2.0 %copy-start = (bf16[14,2,512,128]{3,2,1,0:T(8,128)(2,1)S(1)}, bf16[14,2,512,128]{3,2,1,0:T(8,128)(2,1)}, u32[]{:S(2)}) copy-start(bf16[14,2,512,128]{3,2,1,0:T(8,128)(2,1)} %get-tuple-element.14.cot_ref) | copy-start | bytes 11010052

commit v6 on v5

--- a/solution.py
+++ b/solution.py
@@ -349,12 +349,14 @@
     )
     got = lax.ppermute(give, "dp", swap)
     total = (keep + got.astype(jnp.float32)).astype(jnp.bfloat16)
+    total, cots = lax.optimization_barrier((total, cots))
     sib_cots = lax.ppermute(cots, "dp", swap)
     arrived = lax.all_to_all(
         total, "tensor", split_axis=0, concat_axis=0, tiled=True
     )
+    gate_grad, up_grad = grads_call(own_gate, own_up, first, x_all, cots, sib_cots)
+    arrived, gate_grad, up_grad = lax.optimization_barrier((arrived, gate_grad, up_grad))
     tokens_grad = jnp.sum(arrived.astype(jnp.float32), axis=0).astype(jnp.bfloat16)
-    gate_grad, up_grad = grads_call(own_gate, own_up, first, x_all, cots, sib_cots)
     return (tokens_grad, gate_grad, up_grad)
 
 

time: 152 us -> 125 us (0.82)
  waiting for transfers between devices: 33.1 us -> 4.93 us
  local copies, waits for them, and re-layouts: 2.11 us -> 0.07 us
  Pallas kernels: 104 us -> 106 us
    all_to_all x1, waiting for transfers between devices: 26 us -> 0.01 us  [body(): lax.all_to_all(total, 'tensor', split_axis=0, concat_axis=0, tiled=True)]
    ppermute x1, waiting for transfers between devices: 7.16 us -> 2.29 us  [body(): got = lax.ppermute(give, 'dp', swap)]
    ppermute x1, waiting for transfers between devices: 0.01 us -> 2.64 us  [body(): sib_cots = lax.ppermute(cots, 'dp', swap)]
    pallas_call x1, Pallas kernels: 23.7 us -> 26 us  [grads_call(): pl.pallas_call(functools.partial(grad_kernel, half), grid_spec=pltpu.Pref...]
    unnamed x2 -> x0, local copies, waits for them, and re-layouts: 2.04 us -> none
  transfers between devices with their start and end apart: 3 -> 3, of which waited for: 2 -> 2; matrix products, arithmetic and copies ran while one was open for 2% -> 0% of each run, Pallas kernels for 0% -> 21%
where the time goes in v6:
time: 125 us; the launch traced here: 124 us
  Pallas kernels  106 us (85%)
  other arithmetic  7.71 us (6%)
  waiting for transfers between devices  4.93 us (4%)
  starting transfers between devices  4.41 us (4%)
    pallas_call x1, Pallas kernels, gather_all(): pl.pallas_call(functools.partial(gather_kernel, owners), in_specs=[pl.Blo...  42.6 us
    pallas_call x1, Pallas kernels, slots_call(): pl.pallas_call(functools.partial(slot_kernel, nonzero), grid_spec=pltpu.P...  37.6 us
    pallas_call x1, Pallas kernels, grads_call(): pl.pallas_call(functools.partial(grad_kernel, half), grid_spec=pltpu.Pref...  26 us
    all_to_all x1, starting transfers between devices, body(): lax.all_to_all(total, 'tensor', split_axis=0, concat_axis=0, tiled=True)  3.66 us
    ppermute x1, waiting for transfers between devices, body(): sib_cots = lax.ppermute(cots, 'dp', swap)  2.64 us
  transfers between devices with their start and end apart: 3, of which 2 were waited for; matrix products, arithmetic and copies ran while one was open for 0% of the time, Pallas kernels for 21%

profile of v6, /device:TPU:0, one launch (start us, length us, event | category | flops | bytes accessed | tf_op | source)
XLA Modules:
  0.0 124.0 jit_solution(13515283711442656566)
XLA Ops:
  0.6 0.7 compare_convert_fusion
  1.3 0.7 fusion
  2.0 0.1 pad_add_fusion.where
  2.1 2.2 %multiply_bitcast_fusion.hid_ref = bf16[28,128,128]{2,1,0:T(8,128)(2,1)} fusion(bf16[128,28,128]{2,0,1:T(8,128)(2,1)} %param.8, bf16[28]{0:T(256)(128)(2,1)S(1)} %compare_convert_fusion), kind=kLoop, calls=%fused_computation.1 | loop fusion | flops 458752 | bytes 1835064 | tf_op jit(solution)/shard_map/transpose | solution.py:335
  4.3 42.6 %shard_map.94 = (bf16[4,4,128,1024]{3,2,1,0:T(8,128)(2,1)}, bf16[4,28,128,128]{3,2,1,0:T(8,128)(2,1)}) custom-call(bf16[128,1024]{1,0:T(8,128)(2,1)} %x_ref.1, bf16[28,128,128]{2,1,0:T(8,128)(2,1)} %multiply_bitcast_fusion.hid_ref), custom_call_target="tpu_custom_call" | custom-call | tf_op jit(solution)/shard_map/pallas_call | solution.py:143
  47.0 1.7 %multiply_reduce_fusion = (s32[28,16]{1,0:T(8,128)S(1)}, s32[28,16]{1,0:T(8,128)S(1)}) fusion(s32[112,16]{0,1:T(8,128)} %param.12, s32[28,112]{1,0:T(8,128)S(1)} %fusion, s32[112,16]{0,1:T(8,128)} %param.11), kind=kLoop, calls=%fused_computation.2 | loop fusion | flops 199808 | bytes 30464 | tf_op jit(solution)/shard_map/reduce_sum | solution.py:332
  48.7 37.6 %shard_map.95 = (bf16[14,2,512,128]{3,2,1,0:T(8,128)(2,1)}, f32[4,128,1024]{2,1,0:T(8,128)S(1)}, bf16[4,128,1024]{2,1,0:T(8,128)(2,1)S(1)}) custom-call(s32[28,16]{1,0:T(8,128)S(1)} %get-tuple-element.28.rows_gate, s32[28,16]{1,0:T(8,128)S(1)} %get-tuple-element.27.rows_up, s32[2]{0:T(128)S(1)} %pad_add_fusion.where, ...), custom_call_target="tpu_custom_call" | custom-call | flops 11274289152 | bytes 14680064 | tf_op jit(solution)/shard_map/pallas_call | solution.py:220
  86.3 0.4 collective-permute-start
  86.7 2.3 %collective-permute-done = bf16[4,128,1024]{2,1,0:T(8,128)(2,1)S(1)} collective-permute-done((bf16[4,128,1024]{2,1,0:T(8,128)(2,1)S(1)}, bf16[4,128,1024]{2,1,0:T(8,128)(2,1)S(1)}, u32[]{:S(2)}, u32[]{:S(2)}) %collective-permute-start) | collective-permute-done | bytes 1048608 | tf_op jit(solution)/shard_map/ppermute | solution.py:350
  89.0 1.3 %add_convert_fusion = bf16[4,128,1024]{2,1,0:T(8,128)(2,1)} fusion(f32[4,128,1024]{2,1,0:T(8,128)S(1)} %get-tuple-element.17, bf16[4,128,1024]{2,1,0:T(8,128)(2,1)S(1)} %collective-permute-done), kind=kLoop, calls=%fused_computation | loop fusion | flops 1572864 | bytes 4194304 | tf_op jit(solution)/shard_map/convert_element_type | solution.py:351
  90.3 0.4 collective-permute-start.1
  90.7 3.7 %all-to-all-start = ((bf16[4,128,1024]{2,1,0:T(8,128)(2,1)}), bf16[4,128,1024]{2,1,0:T(8,128)(2,1)S(1)}, u32[]{:S(2)}, u32[]{:S(2)}) async-start(bf16[4,128,1024]{2,1,0:T(8,128)(2,1)} %add_convert_fusion), calls=%async_computation | async-start | bytes 2097152 | tf_op jit(solution)/shard_map/all_to_all | solution.py:354
  94.4 0.1 constant_dynamic-slice_fusion
  94.4 2.6 %collective-permute-done.1.sib_ref = bf16[14,2,512,128]{3,2,1,0:T(8,128)(2,1)} collective-permute-done((bf16[14,2,512,128]{3,2,1,0:T(8,128)(2,1)}, bf16[14,2,512,128]{3,2,1,0:T(8,128)(2,1)}, u32[]{:S(2)}, u32[]{:S(2)}) %collective-permute-start.1) | collective-permute-done | bytes 3670048 | tf_op jit(solution)/shard_map/ppermute | solution.py:353
  97.1 26.0 %shard_map.96 = (bf16[28,4,128,128]{3,2,1,0:T(8,128)(2,1)}, bf16[28,4,128,128]{3,2,1,0:T(8,128)(2,1)}) custom-call(s32[28,4]{1,0:T(8,128)S(1)} %get-tuple-element.30.rows_gate, s32[28,4]{1,0:T(8,128)S(1)} %get-tuple-element.29.rows_up, s32[1]{0:T(128)} %bitcast.1.where, bf16[4,4,128,1024]{3,2,1,0:T(8,128)(2,1)} %get-tuple-element.15.x_ref, ...), custom_call_target="tpu_custom_call" | custom-call | flops 3758096384 | bytes 7340032 | tf_op jit(solution)/shard_map/pallas_call | solution.py:294
  123.1 0.0 all-to-all-done
  123.1 0.9 reduce_sum.32
Async XLA Ops:
  86.3 2.7 %collective-permute-start = (bf16[4,128,1024]{2,1,0:T(8,128)(2,1)S(1)}, bf16[4,128,1024]{2,1,0:T(8,128)(2,1)S(1)}, u32[]{:S(2)}, u32[]{:S(2)}) collective-permute-start(bf16[4,128,1024]{2,1,0:T(8,128)(2,1)S(1)} %get-tuple-element.18), channel_id=1, source_target_pairs={{0,1},{1,0},{2,3},{3,2},{4,5},{5,4},{6,7},{7,6},{8,9},{9,8},{10,11... | collective-permute-start | bytes 3145736 | tf_op jit(solution)/shard_map/ppermute | solution.py:350
  90.3 6.8 %collective-permute-start.1 = (bf16[14,2,512,128]{3,2,1,0:T(8,128)(2,1)}, bf16[14,2,512,128]{3,2,1,0:T(8,128)(2,1)}, u32[]{:S(2)}, u32[]{:S(2)}) collective-permute-start(bf16[14,2,512,128]{3,2,1,0:T(8,128)(2,1)} %get-tuple-element.21.cot_ref), channel_id=1, source_target_pairs={{0,1},{1,0},{2,3},{3,2},{4,5},{5,4},{6,7},{7,6},{8,9},{9,8},{10,11... | collective-permute-start | bytes 11010056 | tf_op jit(solution)/shard_map/ppermute | solution.py:353
  90.7 32.4 %all-to-all-start = ((bf16[4,128,1024]{2,1,0:T(8,128)(2,1)}), bf16[4,128,1024]{2,1,0:T(8,128)(2,1)S(1)}, u32[]{:S(2)}, u32[]{:S(2)}) async-start(bf16[4,128,1024]{2,1,0:T(8,128)(2,1)} %add_convert_fusion), calls=%async_computation | async-start | bytes 2097152 | tf_op jit(solution)/shard_map/all_to_all | solution.py:354
